TPU v7x, 512 devices: a whole 4x8x8 slice. The times are simulated.
512 devices in a mesh: heads: 16 (over z_hi, y), batch: 32 (over x, z_lo, core).
Axes of the slice: x: 4, y: 8, z: 8 (z_hi: 2, z_lo: 4; z = z_hi * 4 + z_lo), core: 2. Of those that a mesh axis runs over, the one named last changes fastest.
Arguments:
- q_latent: bfloat16 [128, 1536], P('batch'), may hold values from -8 to 8
- new_latent: bfloat16 [128, 512], P('batch'), may hold values from -6 to 6
- new_rope: bfloat16 [128, 64], P('batch'), may hold values from -6 to 6
- latent_cache: bfloat16 [128, 1024, 512], P('batch'), may hold values from -8 to 8
- rope_cache: bfloat16 [128, 1024, 64], P('batch'), may hold values from -6 to 6
- lengths: int32 [128], P('batch'), may hold values from 1 to 1024, as said below
- q_up: bfloat16 [6144, 1536], P(('heads', 'batch')), may hold values from -5 to 5
- kv_up: bfloat16 [8192, 512], P(('heads', 'batch')), may hold values from -2 to 2
- out_proj: bfloat16 [7168, 4096], P(('heads', 'batch')), may hold values from -1.5 to 1.5
Outputs:
- attn_out: bfloat16 [128, 7168], P('batch', 'heads')
Inputs may be any that keep to these rules, and one draw needn't show every extreme that they name: `lengths`: every aligned block of 4 rows holds at least one row of length 1024.
All inputs are finite; a program needn't handle non-finite values.
Results may differ from a plain program's by a relative error of at most 0.011.
Values may be sent and summed in bfloat16 or wider, within the bound.
A program may use at most 64 MiB of HBM per device.

v0:
```python
import jax
import jax.numpy as jnp
from jax import lax
from jax.sharding import PartitionSpec as P

HEADS = 32
QR = 1536
KVR = 512
NOPE = 128
ROPE = 64
VDIM = 128


def rotate_half(values, angles):
    half_size = values.shape[-1] // 2
    cosine = jnp.cos(angles)
    sine = jnp.sin(angles)
    first_half = values[..., :half_size]
    second_half = values[..., half_size:]
    return jnp.concatenate(
        [first_half * cosine - second_half * sine, second_half * cosine + first_half * sine],
        axis=-1,
    )


def rope_angles(lengths, width):
    half_size = width // 2
    inverse = 50000.0 ** (-2.0 * jnp.arange(half_size, dtype=jnp.float32) / width)
    return lengths.astype(jnp.float32)[:, None] * inverse[None, :]


def shards(
    q_latent, new_latent, new_rope, latent_cache, rope_cache, lengths, q_up, kv_up, out_proj
):
    head_count = HEADS // lax.axis_size("heads")
    scale_factor = (NOPE + ROPE) ** (-0.5)
    query_rows, kv_rows = (
        lax.all_gather(q_up, "batch", axis=0, tiled=True),
        lax.all_gather(kv_up, "batch", axis=0, tiled=True),
    )
    query_w = query_rows.reshape(head_count, NOPE + ROPE, QR)
    kv_w = kv_rows.reshape(head_count, NOPE + VDIM, KVR)
    value_w = kv_w[:, NOPE:]
    absorbed_q = jnp.einsum(
        "hdc,hdq->hcq", kv_w[:, :NOPE], query_w[:, :NOPE], preferred_element_type=jnp.float32
    ).astype(jnp.bfloat16)
    angles = rope_angles(lengths, ROPE)
    key_new = rotate_half(new_rope.astype(jnp.float32), angles).astype(jnp.bfloat16)
    query_abs = jnp.einsum(
        "rq,hcq->rhc", q_latent, absorbed_q, preferred_element_type=jnp.float32
    ).astype(jnp.bfloat16)
    rope_raw = jnp.einsum(
        "rq,hpq->rhp", q_latent, query_w[:, NOPE:], preferred_element_type=jnp.float32
    )
    query_rope = rotate_half(rope_raw, angles[:, None, :]).astype(jnp.bfloat16)
    scores = jnp.einsum("rhc,rtc->rht", query_abs, latent_cache, preferred_element_type=jnp.float32)
    scores = (
        scores
        + jnp.einsum("rhp,rtp->rht", query_rope, rope_cache, preferred_element_type=jnp.float32)
    ) * scale_factor
    score_new = jnp.einsum("rhc,rc->rh", query_abs, new_latent, preferred_element_type=jnp.float32)
    score_new = (
        score_new
        + jnp.einsum("rhp,rp->rh", query_rope, key_new, preferred_element_type=jnp.float32)
    ) * scale_factor
    valid = jnp.arange(latent_cache.shape[1])[None, :] < lengths[:, None]
    scores = jnp.where(valid[:, None, :], scores, -1e30)
    top_score = jnp.maximum(jnp.max(scores, -1), score_new)
    weights_old = jnp.exp(scores - top_score[..., None])
    weight_new = jnp.exp(score_new - top_score)
    denom = jnp.sum(weights_old, -1) + weight_new
    probs = (weights_old / denom[..., None]).astype(jnp.bfloat16)
    prob_new = (weight_new / denom).astype(jnp.bfloat16)
    context = jnp.einsum("rht,rtc->rhc", probs, latent_cache, preferred_element_type=jnp.float32)
    context = (
        context
        + prob_new.astype(jnp.float32)[..., None] * new_latent.astype(jnp.float32)[:, None, :]
    ).astype(jnp.bfloat16)
    value_out = jnp.einsum(
        "rhc,hvc->rhv", context, value_w, preferred_element_type=jnp.float32
    ).astype(jnp.bfloat16)
    row_count = value_out.shape[0]
    value_flat = value_out.reshape(row_count, -1)
    row_block = lax.all_gather(out_proj, "batch", axis=0, tiled=True)
    head_slice = lax.all_to_all(row_block, "heads", split_axis=1, concat_axis=0, tiled=True)
    partial_out = jnp.einsum(
        "rc,ac->ra", value_flat, head_slice, preferred_element_type=jnp.float32
    )
    return lax.psum_scatter(partial_out, "heads", scatter_dimension=1, tiled=True).astype(
        jnp.bfloat16
    )


def solution(mesh):
    placed = (
        P("batch", None),
        P("batch", None),
        P("batch", None),
        P("batch", None, None),
        P("batch", None, None),
        P("batch"),
        P(("heads", "batch"), None),
        P(("heads", "batch"), None),
        P(("heads", "batch"), None),
    )
    return jax.shard_map(
        shards, mesh=mesh, in_specs=placed, out_specs=P("batch", "heads"), check_vma=False
    )
```

profile of v0, /device:TPU:2, one launch (start us, length us, event | category | flops | bytes accessed | tf_op | source)
XLA Modules:
  0.0 501.1 jit_solution(1967847044607361149)
XLA Ops:
  6.5 0.0 copy-start
  6.5 0.0 all-gather.7.cloned.1.call-start
  6.5 0.7 all-gather.7.cloned.1.call-update
  7.3 72.8 %all-gather.7.cloned.1.call-done = bf16[32,14,4096]{2,1,0:T(8,128)(2,1)} async-done(((bf16[1,14,4096]{2,1,0:T(8,128)(2,1)}), bf16[32,14,4096]{2,1,0:T(8,128)(2,1)}) %all-gather.7.cloned.1.call-update) | async-done | bytes 3670032 | tf_op jit(solution)/shard_map/all_gather | solution.py:84
  80.1 7.2 %all_to_all.14 = bf16[448,16,256]{2,1,0:T(8,128)(2,1)} reshape(bf16[32,14,4096]{2,1,0:T(8,128)(2,1)} %all-gather.7.cloned.1.call-done) | data formatting | bytes 7340032 | tf_op jit(solution)/shard_map/all_to_all | solution.py:85
  87.3 5.2 %copy.26 = bf16[448,16,256]{2,0,1:T(8,128)(2,1)} copy(bf16[448,16,256]{2,1,0:T(8,128)(2,1)} %all_to_all.14) | data formatting | bytes 7340032 | tf_op jit(solution)/shard_map/all_to_all | solution.py:85
  92.5 0.0 copy-start.5
  92.5 0.0 copy-start.6
  92.5 0.0 copy-start.4
  92.5 0.0 copy-start.2
  92.5 0.0 copy-start.3
  92.5 10.3 %all-to-all-start = ((bf16[448,16,256]{2,0,1:T(8,128)(2,1)}), bf16[448,16,256]{2,0,1:T(8,128)(2,1)}, u32[]{:S(2)}, u32[]{:S(2)}) async-start(bf16[448,16,256]{2,0,1:T(8,128)(2,1)} %copy.26), calls=%async_computation | async-start | bytes 7340032 | tf_op jit(solution)/shard_map/all_to_all | solution.py:85
  102.8 0.0 all-gather.5.cloned.1.call-start
  102.9 0.7 all-gather.5.cloned.1.call-update
  103.6 0.0 reduce-scatter.4.cloned.1.call-start
  103.6 0.0 copy-done.5
  103.6 0.0 copy-done.6
  103.7 0.0 copy-done.4
  103.7 0.1 subtract_convert_fusion.1
  103.8 0.1 maximum_bitcast_fusion
  103.9 0.1 iota_compare_fusion
  104.0 0.0 copy-done.2
  104.0 116.1 %all_gather.9 = bf16[512,512]{1,0:T(8,128)(2,1)S(1)} all-gather(bf16[16,512]{1,0:T(8,128)(2,1)S(1)} %copy-done.2), channel_id=1, replica_groups=mesh['heads'=16,'batch'=32] {'batch'}, dimensions={0}, use_global_device_ids=true | all-gather | bytes 540672 | tf_op jit(solution)/shard_map/all_gather | solution.py:39
  220.1 14.4 %all-gather.5.cloned.1.call-done = bf16[32,12,1536]{2,1,0:T(8,128)(2,1)} async-done(((bf16[1,12,1536]{2,1,0:T(8,128)(2,1)}), bf16[32,12,1536]{2,1,0:T(8,128)(2,1)}) %all-gather.5.cloned.1.call-update) | async-done | bytes 1179664 | tf_op jit(solution)/shard_map/all_gather | solution.py:38
  234.5 2.2 reshape.86
  236.7 0.0 copy-done.3
  236.7 0.2 fusion.9
  237.0 0.1 subtract_convert_fusion
  237.0 0.1 pad_maximum_fusion
  237.1 0.1 fusion.27
  237.3 1.8 fusion.5
  239.0 0.0 copy-start.1
  239.0 0.1 fusion.22
  239.2 3.5 fusion.25
  242.7 0.0 copy-done
  242.7 0.3 fusion.34
  243.0 0.2 fusion.15
  243.2 0.0 copy-done.1
  243.2 0.7 fusion.3
  243.9 0.0 all-to-all-done
  243.9 5.1 %convolution_bitcast_fusion = f32[7168,4]{1,0:T(8,128)} fusion(bf16[7168,256]{1,0:T(8,128)(2,1)} %bitcast.14, bf16[2,256,512]{2,1,0:T(8,128)(2,1)S(1)} %bitcast.34, bf16[4,2,512]{2,1,0:T(2,128)(2,1)S(1)} %fusion.3), kind=kOutput, calls=%fused_computation | convolution fusion | flops 15729664 | bytes 4055040
  249.0 0.0 reduce-scatter.4.cloned.1.call-update
  249.1 243.8 %reduce-scatter.4.cloned.1.call-done = f32[448,4]{1,0:T(8,128)} async-done(((f32[7168,4]{1,0:T(8,128)}), f32[448,4]{1,0:T(8,128)}) %reduce-scatter.4.cloned.1.call-update) | async-done | bytes 7184
  492.9 1.6 copy.32
  (6 shorter events, 0.0 us)
Async XLA Ops:
  6.5 236.2 %copy-start = (bf16[4,1024,64]{1,2,0:T(8,128)(2,1)S(1)}, bf16[4,1024,64]{1,2,0:T(8,128)(2,1)}, u32[]{:S(2)}) copy-start(bf16[4,1024,64]{1,2,0:T(8,128)(2,1)} %param.13) | copy-start | bytes 1572868
  6.5 73.6 %all-gather.7.cloned.1.call-start = ((), (), s32[]{:S(2)}) async-start(), calls=%async_computation.3 | async-start | bytes 4325376 | tf_op jit(solution)/shard_map/all_gather | solution.py:84
  92.5 11.1 %copy-start.5 = (bf16[4,64]{1,0:T(4,128)(2,1)S(1)}, bf16[4,64]{1,0:T(4,128)(2,1)}, u32[]{:S(2)}) copy-start(bf16[4,64]{1,0:T(4,128)(2,1)} %param.11) | copy-start | bytes 1540
  92.5 11.2 %copy-start.6 = (s32[4]{0:T(128)S(1)}, s32[4]{0:T(128)}, u32[]{:S(2)}) copy-start(s32[4]{0:T(128)} %param.14) | copy-start | bytes 52
  92.5 11.2 %copy-start.4 = (bf16[4,512]{1,0:T(4,128)(2,1)S(1)}, bf16[4,512]{1,0:T(4,128)(2,1)}, u32[]{:S(2)}) copy-start(bf16[4,512]{1,0:T(4,128)(2,1)} %param.10) | copy-start | bytes 12292
  92.5 11.5 %copy-start.2 = (bf16[16,512]{1,0:T(8,128)(2,1)S(1)}, bf16[16,512]{1,0:T(8,128)(2,1)}, u32[]{:S(2)}) copy-start(bf16[16,512]{1,0:T(8,128)(2,1)} %param.16) | copy-start | bytes 49156
  92.5 144.2 %copy-start.3 = (bf16[4,1536]{1,0:T(4,128)(2,1)S(1)}, bf16[4,1536]{1,0:T(4,128)(2,1)}, u32[]{:S(2)}) copy-start(bf16[4,1536]{1,0:T(4,128)(2,1)} %param.9) | copy-start | bytes 36868
  92.5 151.4 %all-to-all-start = ((bf16[448,16,256]{2,0,1:T(8,128)(2,1)}), bf16[448,16,256]{2,0,1:T(8,128)(2,1)}, u32[]{:S(2)}, u32[]{:S(2)}) async-start(bf16[448,16,256]{2,0,1:T(8,128)(2,1)} %copy.26), calls=%async_computation | async-start | bytes 7340032 | tf_op jit(solution)/shard_map/all_to_all | solution.py:85
  102.8 131.7 %all-gather.5.cloned.1.call-start = ((), (), s32[]{:S(2)}) async-start(), calls=%async_computation.2 | async-start | bytes 1622016 | tf_op jit(solution)/shard_map/all_gather | solution.py:38
  103.6 389.3 %reduce-scatter.4.cloned.1.call-start = ((), (), s32[]{:S(2)}) async-start(), calls=%async_computation.4 | async-start | bytes 3899392
  239.0 4.2 copy-start.1
Sparse Core Ops, SparseCore 0:
  9.5 70.5 all-gather.6
  105.8 128.6 all-gather.4
  249.2 243.6 reduce-scatter.3
where the time goes:
time: 502 us; the launch traced here: 501 us
  waiting for transfers between devices  332 us (66%)
  blocking collectives  116 us (23%)
  local copies, waits for them, and re-layouts  16.3 us (3%)
  between operations  13.2 us (3%)
  matrix products  11.9 us (2%)
  starting transfers between devices  10.4 us (2%)
    unnamed x4, waiting for transfers between devices  245 us
    all_gather x1, blocking collectives, shards(): lax.all_gather(kv_up, 'batch', axis=0, tiled=True)  116 us
    all_gather x1, waiting for transfers between devices, shards(): row_block = lax.all_gather(out_proj, 'batch', axis=0, tiled=True)  72.8 us
    all_gather x1, waiting for transfers between devices, shards(): lax.all_gather(q_up, 'batch', axis=0, tiled=True)  14.4 us
    all_to_all x2, local copies, waits for them, and re-layouts, shards(): lax.all_to_all(row_block, 'heads', split_axis=1, concat_axis=0, tiled=True)  12.4 us
    all_to_all x1, starting transfers between devices, shards(): lax.all_to_all(row_block, 'heads', split_axis=1, concat_axis=0, tiled=True)  10.3 us
  transfers between devices with their start and end apart: 4, of which 3 were waited for; matrix products, arithmetic and copies ran while one was open for 2% of the time, Pallas kernels for 0%

commit v1 on v0

v1 whole, which is shorter than its diff:
```python
import functools
import math

import jax
import jax.numpy as jnp
from jax import lax
from jax.experimental import pallas as pl
from jax.experimental.pallas import tpu as pltpu
from jax.sharding import PartitionSpec as P

QR = 1536
KVR = 512
NOPE = 128
ROPE = 64
CACHE = 1024
QROWS = 12
SLOT = 16
XS, ZS = 4, 4
HS = 16
QC = QR // 4
OUT_K = 4096
F32 = jnp.float32
BF16 = jnp.bfloat16
NT = (((1,), (1,)), ((), ()))


def dot_nt(a, b):
    return lax.dot_general(a, b, NT, preferred_element_type=F32)


def dot_nn(a, b):
    return jnp.dot(a, b, preferred_element_type=F32)


def kernel(
    ql_hbm, nl_hbm, nr_hbm, lat_hbm, rope_hbm, len_hbm, qup_hbm, kvup_hbm, outp_hbm, y_ref,
    ql_in, nl_in, nr_in, len_in, qup_in, outp_in, lat, rope,
    qbuf, qlbuf, qsend, qrecv, kvbuf, wbuf, sel, sel_out, vx, vh, ysend, yrecv,
    in_sem, q_send, q_recv, ql_send, ql_recv, qx_send, qx_recv, kvz_send, kvb_send, kv_recv,
    w_send, w_recv, vx_send, vx_recv, vh_send, vh_recv, y_send, y_recv,
):
    h = lax.axis_index("heads")
    b = lax.axis_index("batch")
    x, z, c = b // 8, (b // 2) % 4, b % 2

    def index(xx, zz, cc):
        return xx * 8 + zz * 2 + cc

    zk = [z, z + 1 - 2 * (z % 2), (z + 2) % 4, 3 - z]
    xr, xl, xo = (x + 1) % 4, (x + 3) % 4, (x + 2) % 4
    right, left, sibling = index(xr, z, c), index(xl, z, c), index(x, z, 1 - c)
    mine, theirs = x * 2 + c, x * 2 + 1 - c
    own = z * 2 + c

    loads = [
        pltpu.make_async_copy(source, target, in_sem.at[i])
        for i, (source, target) in enumerate(
            [
                (qup_hbm, qup_in), (ql_hbm, ql_in), (kvup_hbm, kvbuf.at[mine, z]),
                (nl_hbm, nl_in), (nr_hbm, nr_in), (len_hbm, len_in), (outp_hbm, outp_in),
                (lat_hbm, lat), (rope_hbm, rope),
            ]
        )
    ]
    for load in loads:
        load.start()

    barrier = pltpu.get_barrier_semaphore()

    def greet(target):
        pl.semaphore_signal(barrier, inc=1, device_id={"batch": target})

    greet(right)
    greet(left)
    greet(sibling)
    for k in range(1, ZS):
        greet(index(x, zk[k], c))
        greet(index(x, zk[k], 1 - c))

    @pl.loop(1, HS)
    def _(i):
        pl.semaphore_signal(barrier, inc=1, device_id={"heads": (h + i) % HS})

    loads[0].wait()
    qbuf[x, :, :] = jnp.concatenate([qup_in[...], jnp.zeros((SLOT - QROWS, QR), BF16)], axis=0)
    loads[1].wait()
    ql_own = ql_in[...].astype(F32)
    qlbuf[own, :, :] = jnp.concatenate(
        [ql_own[:, j * QC: (j + 1) * QC] for j in range(4)], axis=0
    ).astype(BF16)
    loads[2].wait()

    pl.semaphore_wait(barrier, 2 + 1 + 6 + HS - 1)

    def remote(source, target, send_sem, recv_sem, device):
        return pltpu.make_async_remote_copy(
            src_ref=source, dst_ref=target, send_sem=send_sem, recv_sem=recv_sem,
            device_id=device,
        )

    def push(ref, send_sem, recv_sem, target):
        remote(ref, ref, send_sem, recv_sem, {"batch": target}).start()

    def arrive(ref, recv_sem):
        pltpu.make_async_copy(ref, ref, recv_sem).wait()

    for target in (right, left):
        push(qbuf.at[x], q_send.at[0], q_recv.at[x, 0], target)
    for k in range(1, ZS):
        push(kvbuf.at[mine, z], kvz_send.at[0], kv_recv.at[z], index(x, zk[k], c))
    for k in range(1, ZS):
        push(qlbuf.at[own], ql_send.at[0], ql_recv.at[own], index(x, zk[k], c))
    push(qlbuf.at[own], ql_send.at[0], ql_recv.at[own], sibling)

    @pl.loop(0, 32)
    def _(t):
        x_t = t % 4
        first_row = QROWS * ((x_t % 2) * 8 + (t // 8) * 2 + (t // 4) % 2)
        shape = (SLOT, 2 * NOPE + 2 * ROPE)
        within = lax.broadcasted_iota(jnp.int32, shape, 0)
        col = lax.broadcasted_iota(jnp.int32, shape, 1)
        row = within + first_row
        nope = (row < NOPE) & (col == row + (x_t // 2) * NOPE)
        rotary = row - NOPE
        swapped = (rotary + ROPE // 2) % ROPE
        rope_at = (row >= NOPE) & (
            (col == 2 * NOPE + rotary) | (col == 2 * NOPE + ROPE + swapped)
        )
        block = jnp.where((within < QROWS) & (nope | rope_at), 1.0, 0.0).astype(BF16)
        sel[pl.ds(pl.multiple_of(t * SLOT, SLOT), SLOT), :] = block

    arrive(qbuf.at[xl], q_recv.at[xl, 0])
    push(qbuf.at[xl, :, pl.ds(0, QR // 2)], q_send.at[0], q_recv.at[xl, 0], right)
    arrive(qbuf.at[xr], q_recv.at[xr, 0])
    push(qbuf.at[xr, :, pl.ds(QR // 2, QR // 2)], q_send.at[0], q_recv.at[xr, 1], left)

    for k in range(1, ZS):
        arrive(kvbuf.at[mine, zk[k]], kv_recv.at[zk[k]])
    for target in (right, left):
        push(kvbuf.at[mine], kvb_send.at[0], kv_recv.at[4 + x], target)
    push(kvbuf.at[mine], kvb_send.at[0], kv_recv.at[4 + x], sibling)
    for k in range(1, ZS):
        slot = zk[k] * 2 + c
        arrive(qlbuf.at[slot], ql_recv.at[slot])
        push(qlbuf.at[slot], ql_send.at[0], ql_recv.at[slot], sibling)

    loads[6].wait()
    wbuf[mine, :, :] = jnp.concatenate([outp_in[...], jnp.zeros((2, OUT_K), BF16)], axis=0)

    from_left, from_right, from_far = xl * 2 + c, xr * 2 + c, xo * 2 + c
    arrive(kvbuf.at[from_left], kv_recv.at[4 + xl])
    push(kvbuf.at[from_left, pl.ds(0, 2)], kvb_send.at[0], kv_recv.at[12], right)
    push(kvbuf.at[from_left], kvb_send.at[0], kv_recv.at[8 + xl], sibling)
    arrive(kvbuf.at[from_right], kv_recv.at[4 + xr])
    push(kvbuf.at[from_right, pl.ds(2, 2)], kvb_send.at[0], kv_recv.at[13], left)
    push(kvbuf.at[from_right], kvb_send.at[0], kv_recv.at[8 + xr], sibling)

    for target in (right, left, sibling):
        push(wbuf.at[mine], w_send.at[0], w_recv.at[mine, 0], target)

    arrive(qbuf.at[xo, :, pl.ds(0, QR // 2)], q_recv.at[xo, 0])
    arrive(qbuf.at[xo, :, pl.ds(QR // 2, QR // 2)], q_recv.at[xo, 1])
    for zz in range(ZS):
        slot = zz * 2 + 1 - c
        arrive(qlbuf.at[slot], ql_recv.at[slot])
    ql_rows = qlbuf[...].reshape(8 * SLOT, QC)
    block_of = (lax.broadcasted_iota(jnp.int32, (8 * SLOT, XS * SLOT), 0) // 4) % 4
    partial = jnp.zeros((8 * SLOT, XS * SLOT), F32)
    for j in range(4):
        columns = qbuf[:, :, j * QC: (j + 1) * QC].reshape(XS * SLOT, QC)
        partial = jnp.where(block_of == j, dot_nt(ql_rows, columns), partial)
    partial = partial.reshape(8, SLOT, XS * SLOT)
    partial = partial[:, 0:8] + partial[:, 8:16]
    partial = jnp.concatenate([partial, partial], axis=2)
    lane_of = lax.broadcasted_iota(jnp.int32, (8, 8, 128), 2)
    qsend[...] = jnp.where(lane_of // 64 == c, partial, 0.0)
    for k in range(1, ZS):
        for cc in (c, 1 - c):
            slot = zk[k] * 2 + cc
            remote(
                qsend.at[slot], qrecv.at[own], qx_send.at[0], qx_recv.at[own],
                {"batch": index(x, zk[k], cc)},
            ).start()
    remote(
        qsend.at[z * 2 + 1 - c], qrecv.at[own], qx_send.at[0], qx_recv.at[own], {"batch": sibling}
    ).start()
    qrecv[own, :, :] = qsend[own]

    arrive(kvbuf.at[from_far, pl.ds(0, 2)], kv_recv.at[12])
    arrive(kvbuf.at[from_far, pl.ds(2, 2)], kv_recv.at[13])
    push(kvbuf.at[from_far], kvb_send.at[0], kv_recv.at[8 + xo], sibling)

    row8 = lax.broadcasted_iota(jnp.int32, (8, 1), 0)
    row_of = row8 % 4
    low = row8 < 4
    for load in loads[3:6]:
        load.wait()
    length = jnp.zeros((8, 1), jnp.int32)
    for r in range(4):
        length = jnp.where(row_of == r, len_in[r], length)

    lane64 = lax.broadcasted_iota(jnp.int32, (8, ROPE), 1)
    inverse = jnp.exp((lane64 % (ROPE // 2)).astype(F32) * (-2.0 * math.log(50000.0) / ROPE))
    angles = length.astype(F32) * inverse
    cosine = jnp.cos(angles)
    sine = jnp.sin(angles)
    sine = jnp.where(lane64 < ROPE // 2, -sine, sine)

    def twice(values):
        return jnp.concatenate([values, values], axis=0)

    nr8 = twice(nr_in[...].astype(F32))
    nr_swapped = jnp.concatenate([nr8[:, ROPE // 2:], nr8[:, : ROPE // 2]], axis=1)
    key_new = (nr8 * cosine + nr_swapped * sine).astype(BF16).astype(F32)
    nl8 = twice(nl_in[...].astype(F32))

    for k in range(1, ZS):
        for cc in (c, 1 - c):
            slot = zk[k] * 2 + cc
            arrive(qrecv.at[slot], qx_recv.at[slot])
    arrive(qrecv.at[z * 2 + 1 - c], qx_recv.at[z * 2 + 1 - c])
    pieces = []
    for zz in range(ZS):
        piece = qrecv[2 * zz] + qrecv[2 * zz + 1]
        pieces.append(piece + pltpu.roll(piece, 4, 0))
    q_all = jnp.concatenate(pieces, axis=1)
    lane_q = lax.broadcasted_iota(jnp.int32, (8, 512), 1)
    q_all = jnp.where((lane_q % 64 < 32) == low, q_all, 0.0)
    q_hi = q_all.astype(BF16)
    q_lo = (q_all - q_hi.astype(F32)).astype(BF16)
    selection = sel[...]
    q_sel = dot_nn(q_hi, selection) + dot_nn(q_lo, selection)
    q_nope = q_sel[:, 0: 2 * NOPE].astype(BF16)
    query_rope = (
        q_sel[:, 2 * NOPE: 2 * NOPE + ROPE] * cosine + q_sel[:, 2 * NOPE + ROPE:] * sine
    ).astype(BF16)

    arrive(kvbuf.at[theirs], kv_recv.at[4 + x])
    for xx in (xl, xr, xo):
        block = xx * 2 + 1 - c
        arrive(kvbuf.at[block], kv_recv.at[8 + xx])

    def kv_rows(xx):
        return jnp.concatenate(
            [kvbuf[xx * 2 + cc, zz] for zz in range(ZS) for cc in range(2)], axis=0
        )

    query_abs = (
        dot_nn(q_nope[:, :NOPE], kv_rows(0)) + dot_nn(q_nope[:, NOPE:], kv_rows(2))
    ).astype(BF16)

    loads[7].wait()
    loads[8].wait()
    scale = (NOPE + ROPE) ** (-0.5)
    scores = jnp.zeros((8, CACHE), F32)
    for r in range(4):
        of_row = dot_nt(query_abs, lat[r]) + dot_nn(query_rope, rope[r])
        scores = jnp.where(row_of == r, of_row, scores)
    score_new = scale * (
        jnp.sum(query_abs.astype(F32) * nl8, axis=1, keepdims=True)
        + jnp.sum(query_rope.astype(F32) * key_new, axis=1, keepdims=True)
    )
    position = lax.broadcasted_iota(jnp.int32, (8, CACHE), 1)
    scores = jnp.where(position < length, scores * scale, -1e30)
    top = jnp.maximum(jnp.max(scores, axis=1, keepdims=True), score_new)
    old = jnp.exp(scores - top)
    new = jnp.exp(score_new - top)
    denom = jnp.sum(old, axis=1, keepdims=True) + new
    probs = (old / denom).astype(BF16)
    prob_new = (new / denom).astype(BF16).astype(F32)
    context = jnp.zeros((8, KVR), F32)
    for r in range(4):
        context = jnp.where(row_of == r, dot_nn(probs, lat[r]), context)
    context = (context + prob_new * nl8).astype(BF16)
    value = jnp.where(low, dot_nt(context, kv_rows(1)), dot_nt(context, kv_rows(3)))
    vx[z, :, :] = value.astype(BF16).astype(F32)

    for k in range(1, ZS):
        push(vx.at[z], vx_send.at[0], vx_recv.at[z], index(x, zk[k], c))

    arrive(wbuf.at[from_left], w_recv.at[from_left, 0])
    push(
        wbuf.at[from_left, :, pl.ds(0, OUT_K // 2)], w_send.at[0], w_recv.at[from_left, 0], right
    )
    push(wbuf.at[from_left], w_send.at[0], w_recv.at[from_left, 0], sibling)
    arrive(wbuf.at[from_right], w_recv.at[from_right, 0])
    push(
        wbuf.at[from_right, :, pl.ds(OUT_K // 2, OUT_K // 2)], w_send.at[0],
        w_recv.at[from_right, 1], left,
    )
    push(wbuf.at[from_right], w_send.at[0], w_recv.at[from_right, 0], sibling)

    for k in range(1, ZS):
        arrive(vx.at[zk[k]], vx_recv.at[zk[k]])
    vh[h, :, :] = vx[...].reshape(32, 128).astype(BF16)

    @pl.loop(1, HS)
    def _(i):
        remote(
            vh.at[h], vh.at[h], vh_send.at[0], vh_recv.at[h], {"heads": (h + i) % HS}
        ).start()

    arrive(wbuf.at[from_far, :, pl.ds(0, OUT_K // 2)], w_recv.at[from_far, 0])
    arrive(wbuf.at[from_far, :, pl.ds(OUT_K // 2, OUT_K // 2)], w_recv.at[from_far, 1])
    push(wbuf.at[from_far], w_send.at[0], w_recv.at[from_far, 0], sibling)

    @pl.loop(0, 32)
    def _(t):
        start = (((t // 2) % 4) * 8 + (t // 8) * 2 + t % 2) * 14
        col = lax.broadcasted_iota(jnp.int32, (SLOT, 448), 1) - start
        row = lax.broadcasted_iota(jnp.int32, (SLOT, 448), 0)
        block = jnp.where((col == row) & (row < 14), 1.0, 0.0).astype(BF16)
        sel_out[pl.ds(pl.multiple_of(t * SLOT, SLOT), SLOT), :] = block

    for xx in (x, xl, xr, xo):
        block = xx * 2 + 1 - c
        arrive(wbuf.at[block], w_recv.at[block, 0])

    @pl.loop(1, HS)
    def _(i):
        other = (h + i) % HS
        arrive(vh.at[other], vh_recv.at[other])

    row32 = lax.broadcasted_iota(jnp.int32, (32, 128), 0)
    is_low = (row32 % 8) < 4
    zero = jnp.zeros((32, 128), BF16)
    chunks = []
    for hh in range(HS):
        block = vh[hh]
        chunks.append(jnp.where(is_low, block, zero))
        chunks.append(jnp.where(is_low, zero, block))
    y_all = dot_nt(jnp.concatenate(chunks, axis=1), wbuf[...].reshape(8 * SLOT, OUT_K))
    ysend[...] = y_all.reshape(ZS, 8, 128)

    for k in range(1, ZS):
        remote(
            ysend.at[zk[k]], yrecv.at[z], y_send.at[0], y_recv.at[z],
            {"batch": index(x, zk[k], c)},
        ).start()
    yrecv[z, :, :] = ysend[z]
    for k in range(1, ZS):
        arrive(yrecv.at[zk[k]], y_recv.at[zk[k]])
    pieces = []
    for zz in range(ZS):
        piece = yrecv[zz]
        pieces.append(piece + pltpu.roll(piece, 4, 0))
    summed = jnp.concatenate(pieces, axis=1).astype(BF16)
    y_ref[...] = dot_nn(summed, sel_out[...])[0:4]

    for ref, sem in (
        (qbuf.at[0:3], q_send), (kvbuf.at[0, 0:3], kvz_send), (kvbuf.at[0:7], kvb_send),
        (qlbuf.at[0:7], ql_send), (qsend.at[0:7], qx_send), (wbuf.at[0:7], w_send),
        (vx.at[0:3], vx_send), (vh.at[0:15], vh_send), (ysend.at[0:3], y_send),
    ):
        arrive(ref, sem.at[0])


def shards(
    q_latent, new_latent, new_rope, latent_cache, rope_cache, lengths, q_up, kv_up, out_proj
):
    hbm = pl.BlockSpec(memory_space=pltpu.HBM)
    dma = pltpu.SemaphoreType.DMA
    return pl.pallas_call(
        kernel,
        out_shape=jax.ShapeDtypeStruct((4, 448), F32),
        in_specs=[hbm] * 9,
        out_specs=pl.BlockSpec(memory_space=pltpu.VMEM),
        scratch_shapes=[
            pltpu.VMEM((4, QR), BF16),
            pltpu.VMEM((4, KVR), BF16),
            pltpu.VMEM((4, ROPE), BF16),
            pltpu.SMEM((4,), jnp.int32),
            pltpu.VMEM((QROWS, QR), BF16),
            pltpu.VMEM((14, OUT_K), BF16),
            pltpu.VMEM((4, CACHE, KVR), BF16),
            pltpu.VMEM((4, ROPE, CACHE), BF16),
            pltpu.VMEM((XS, SLOT, QR), BF16),
            pltpu.VMEM((8, SLOT, QC), BF16),
            pltpu.VMEM((8, 8, 128), F32),
            pltpu.VMEM((8, 8, 128), F32),
            pltpu.VMEM((8, ZS, SLOT, KVR), BF16),
            pltpu.VMEM((8, SLOT, OUT_K), BF16),
            pltpu.VMEM((512, 2 * NOPE + 2 * ROPE), BF16),
            pltpu.VMEM((512, 448), BF16),
            pltpu.VMEM((ZS, 8, 128), F32),
            pltpu.VMEM((HS, 32, 128), BF16),
            pltpu.VMEM((ZS, 8, 128), F32),
            pltpu.VMEM((ZS, 8, 128), F32),
            dma((9,)),
            dma((1,)), dma((XS, 2)),
            dma((1,)), dma((8,)),
            dma((1,)), dma((8,)),
            dma((1,)), dma((1,)), dma((14,)),
            dma((1,)), dma((8, 2)),
            dma((1,)), dma((ZS,)),
            dma((1,)), dma((HS,)),
            dma((1,)), dma((ZS,)),
        ],
        compiler_params=pltpu.CompilerParams(
            collective_id=0, has_side_effects=True, vmem_limit_bytes=60 * 2**20
        ),
        cost_estimate=pl.CostEstimate(
            flops=4 * 10**8, bytes_accessed=5 * 10**6, transcendentals=10**4
        ),
    )(
        q_latent, new_latent, new_rope, latent_cache, jnp.swapaxes(rope_cache, 1, 2), lengths,
        q_up, kv_up, out_proj,
    ).astype(BF16)


def solution(mesh):
    placed = (
        P("batch", None),
        P("batch", None),
        P("batch", None),
        P("batch", None, None),
        P("batch", None, None),
        P("batch"),
        P(("heads", "batch"), None),
        P(("heads", "batch"), None),
        P(("heads", "batch"), None),
    )
    return jax.shard_map(
        shards, mesh=mesh, in_specs=placed, out_specs=P("batch", "heads"), check_vma=False
    )
```

time: 502 us -> 47.5 us (0.09)
  the two profiles are of different devices: /device:TPU:2 before, /device:TPU:8 now
where the time goes in v1:
time: 47.5 us; the launch traced here: 47.4 us
  Pallas kernels  46.1 us (97%)
  other arithmetic  1.29 us (3%)
    pallas_call x1, Pallas kernels, shards(): pl.pallas_call(kernel, out_shape=jax.ShapeDtypeStruct((4, 448), F32), in_...  46.1 us
    convert_element_type x1, other arithmetic, shards(): return pl.pallas_call(kernel, out_shape=jax.ShapeDtypeStruct((4, 448), F3...  1.29 us

profile of v1, /device:TPU:8, one launch (start us, length us, event | category | flops | bytes accessed | tf_op | source)
XLA Modules:
  0.0 47.4 jit_solution(4890763258982943151)
XLA Ops:
  0.0 46.1 %shard_map.91 = f32[4,448]{1,0:T(4,128)} custom-call(bf16[4,1536]{1,0:T(4,128)(2,1)} %ql_hbm.1, bf16[4,512]{1,0:T(4,128)(2,1)} %nl_hbm.1, bf16[4,64]{1,0:T(4,128)(2,1)} %nr_hbm.1, bf16[4,1024,512]{2,1,0:T(8,128)(2,1)} %lat_hbm.1, bf16[4,64,1024]{2,1,0:T(8,128)(2,1)} %bitcast.1, s32[4]{0:T(128)} %len_hbm.1, bf16[12,1536]{1,0:T(8,128)(2,1)} %qup_hbm.1, ...), custom_call_target="tpu_custom_call" | custom-call | flops 400000000 | bytes 5000000 | tf_op jit(solution)/shard_map/pallas_call | solution.py:363
  46.1 1.3 %convert_element_type.3 = bf16[4,448]{1,0:T(4,128)(2,1)} convert(f32[4,448]{1,0:T(4,128)} %shard_map.91) | non-fusion elementwise | flops 1792 | bytes 10752 | tf_op jit(solution)/shard_map/convert_element_type | solution.py:408

commit v2 on v1

--- a/solution.py
+++ b/solution.py
@@ -16,7 +16,7 @@
 QROWS = 12
 SLOT = 16
 XS, ZS = 4, 4
-HS = 16
+YS = 8
 QC = QR // 4
 OUT_K = 4096
 F32 = jnp.float32
@@ -42,6 +42,7 @@
     h = lax.axis_index("heads")
     b = lax.axis_index("batch")
     x, z, c = b // 8, (b // 2) % 4, b % 2
+    y, up = h % YS, h // YS
 
     def index(xx, zz, cc):
         return xx * 8 + zz * 2 + cc
@@ -70,16 +71,22 @@
     def greet(target):
         pl.semaphore_signal(barrier, inc=1, device_id={"batch": target})
 
+    across = (1 - up) * YS + y
+    for k in range(ZS):
+        pl.semaphore_signal(
+            barrier, inc=1, device_id={"heads": across, "batch": index(x, zk[k], c)}
+        )
+
+    @pl.loop(1, YS)
+    def _(i):
+        pl.semaphore_signal(barrier, inc=1, device_id={"heads": up * YS + (y + i) % YS})
+
+    for k in range(1, ZS):
+        greet(index(x, zk[k], c))
+        greet(index(x, zk[k], 1 - c))
     greet(right)
     greet(left)
     greet(sibling)
-    for k in range(1, ZS):
-        greet(index(x, zk[k], c))
-        greet(index(x, zk[k], 1 - c))
-
-    @pl.loop(1, HS)
-    def _(i):
-        pl.semaphore_signal(barrier, inc=1, device_id={"heads": (h + i) % HS})
 
     loads[0].wait()
     qbuf[x, :, :] = jnp.concatenate([qup_in[...], jnp.zeros((SLOT - QROWS, QR), BF16)], axis=0)
@@ -90,7 +97,7 @@
     ).astype(BF16)
     loads[2].wait()
 
-    pl.semaphore_wait(barrier, 2 + 1 + 6 + HS - 1)
+    pl.semaphore_wait(barrier, ZS + YS - 1 + 6 + 2 + 1)
 
     def remote(source, target, send_sem, recv_sem, device):
         return pltpu.make_async_remote_copy(
@@ -273,10 +280,19 @@
         context = jnp.where(row_of == r, dot_nn(probs, lat[r]), context)
     context = (context + prob_new * nl8).astype(BF16)
     value = jnp.where(low, dot_nt(context, kv_rows(1)), dot_nt(context, kv_rows(3)))
-    vx[z, :, :] = value.astype(BF16).astype(F32)
-
-    for k in range(1, ZS):
-        push(vx.at[z], vx_send.at[0], vx_recv.at[z], index(x, zk[k], c))
+    z_of_8 = up * ZS + z
+    vx[z_of_8, :, :] = value.astype(BF16).astype(F32)
+
+    def vx_push(heads, k):
+        remote(
+            vx.at[z_of_8], vx.at[z_of_8], vx_send.at[0], vx_recv.at[z_of_8],
+            {"heads": heads, "batch": index(x, zk[k], c)},
+        ).start()
+
+    for k in range(ZS):
+        vx_push(across, k)
+    for k in range(1, ZS):
+        vx_push(h, k)
 
     arrive(wbuf.at[from_left], w_recv.at[from_left, 0])
     push(
@@ -291,13 +307,16 @@
     push(wbuf.at[from_right], w_send.at[0], w_recv.at[from_right, 0], sibling)
 
     for k in range(1, ZS):
-        arrive(vx.at[zk[k]], vx_recv.at[zk[k]])
-    vh[h, :, :] = vx[...].reshape(32, 128).astype(BF16)
-
-    @pl.loop(1, HS)
-    def _(i):
+        arrive(vx.at[up * ZS + zk[k]], vx_recv.at[up * ZS + zk[k]])
+    for k in range(ZS):
+        slot = (1 - up) * ZS + zk[k]
+        arrive(vx.at[slot], vx_recv.at[slot])
+    vh[y, :, :] = vx[...].reshape(64, 128).astype(BF16)
+
+    for i in (4, 3, 5, 2, 6, 1, 7):
         remote(
-            vh.at[h], vh.at[h], vh_send.at[0], vh_recv.at[h], {"heads": (h + i) % HS}
+            vh.at[y], vh.at[y], vh_send.at[0], vh_recv.at[y],
+            {"heads": up * YS + (y + i) % YS},
         ).start()
 
     arrive(wbuf.at[from_far, :, pl.ds(0, OUT_K // 2)], w_recv.at[from_far, 0])
@@ -316,17 +335,16 @@
         block = xx * 2 + 1 - c
         arrive(wbuf.at[block], w_recv.at[block, 0])
 
-    @pl.loop(1, HS)
-    def _(i):
-        other = (h + i) % HS
+    for i in (1, 7, 2, 6, 3, 5, 4):
+        other = (y + i) % YS
         arrive(vh.at[other], vh_recv.at[other])
 
     row32 = lax.broadcasted_iota(jnp.int32, (32, 128), 0)
     is_low = (row32 % 8) < 4
     zero = jnp.zeros((32, 128), BF16)
     chunks = []
-    for hh in range(HS):
-        block = vh[hh]
+    for hh in range(2 * YS):
+        block = vh[hh % YS, hh // YS * 32: hh // YS * 32 + 32]
         chunks.append(jnp.where(is_low, block, zero))
         chunks.append(jnp.where(is_low, zero, block))
     y_all = dot_nt(jnp.concatenate(chunks, axis=1), wbuf[...].reshape(8 * SLOT, OUT_K))
@@ -350,7 +368,7 @@
     for ref, sem in (
         (qbuf.at[0:3], q_send), (kvbuf.at[0, 0:3], kvz_send), (kvbuf.at[0:7], kvb_send),
         (qlbuf.at[0:7], ql_send), (qsend.at[0:7], qx_send), (wbuf.at[0:7], w_send),
-        (vx.at[0:3], vx_send), (vh.at[0:15], vh_send), (ysend.at[0:3], y_send),
+        (vx.at[0:7], vx_send), (vh.at[0:7], vh_send), (ysend.at[0:3], y_send),
     ):
         arrive(ref, sem.at[0])
 
@@ -382,8 +400,8 @@
             pltpu.VMEM((8, SLOT, OUT_K), BF16),
             pltpu.VMEM((512, 2 * NOPE + 2 * ROPE), BF16),
             pltpu.VMEM((512, 448), BF16),
-            pltpu.VMEM((ZS, 8, 128), F32),
-            pltpu.VMEM((HS, 32, 128), BF16),
+            pltpu.VMEM((2 * ZS, 8, 128), F32),
+            pltpu.VMEM((YS, 64, 128), BF16),
             pltpu.VMEM((ZS, 8, 128), F32),
             pltpu.VMEM((ZS, 8, 128), F32),
             dma((9,)),
@@ -392,8 +410,8 @@
             dma((1,)), dma((8,)),
             dma((1,)), dma((1,)), dma((14,)),
             dma((1,)), dma((8, 2)),
-            dma((1,)), dma((ZS,)),
-            dma((1,)), dma((HS,)),
+            dma((1,)), dma((2 * ZS,)),
+            dma((1,)), dma((YS,)),
             dma((1,)), dma((ZS,)),
         ],
         compiler_params=pltpu.CompilerParams(

time: 47.5 us -> 46.1 us (0.971)
  the two profiles are of different devices: /device:TPU:8 before, /device:TPU:2 now
where the time goes in v2:
time: 46.1 us; the launch traced here: 46 us
  Pallas kernels  44.7 us (97%)
  other arithmetic  1.29 us (3%)
    pallas_call x1, Pallas kernels, shards(): pl.pallas_call(kernel, out_shape=jax.ShapeDtypeStruct((4, 448), F32), in_...  44.7 us
    convert_element_type x1, other arithmetic, shards(): return pl.pallas_call(kernel, out_shape=jax.ShapeDtypeStruct((4, 448), F3...  1.29 us

profile of v2, /device:TPU:2, one launch (start us, length us, event | category | flops | bytes accessed | tf_op | source)
XLA Modules:
  0.0 46.0 jit_solution(2026089271410791434)
XLA Ops:
  0.0 44.7 %shard_map.91 = f32[4,448]{1,0:T(4,128)} custom-call(bf16[4,1536]{1,0:T(4,128)(2,1)} %ql_hbm.1, bf16[4,512]{1,0:T(4,128)(2,1)} %nl_hbm.1, bf16[4,64]{1,0:T(4,128)(2,1)} %nr_hbm.1, bf16[4,1024,512]{2,1,0:T(8,128)(2,1)} %lat_hbm.1, bf16[4,64,1024]{2,1,0:T(8,128)(2,1)} %bitcast.1, s32[4]{0:T(128)} %len_hbm.1, bf16[12,1536]{1,0:T(8,128)(2,1)} %qup_hbm.1, ...), custom_call_target="tpu_custom_call" | custom-call | flops 400000000 | bytes 5000000 | tf_op jit(solution)/shard_map/pallas_call | solution.py:381
  44.7 1.3 %convert_element_type.3 = bf16[4,448]{1,0:T(4,128)(2,1)} convert(f32[4,448]{1,0:T(4,128)} %shard_map.91) | non-fusion elementwise | flops 1792 | bytes 10752 | tf_op jit(solution)/shard_map/convert_element_type | solution.py:426

commit v3 on v2

--- a/solution.py
+++ b/solution.py
@@ -63,9 +63,6 @@
             ]
         )
     ]
-    for load in loads:
-        load.start()
-
     barrier = pltpu.get_barrier_semaphore()
 
     def greet(target):
@@ -88,33 +85,35 @@
     greet(left)
     greet(sibling)
 
+    for i in (2, 0, 1, 3, 4, 5, 6, 7, 8):
+        loads[i].start()
+    loads[2].wait()
+    pl.semaphore_wait(barrier, ZS + YS - 1 + 6 + 2 + 1)
+
+    def remote(source, target, send_sem, recv_sem, device):
+        return pltpu.make_async_remote_copy(
+            src_ref=source, dst_ref=target, send_sem=send_sem, recv_sem=recv_sem,
+            device_id=device,
+        )
+
+    def push(ref, send_sem, recv_sem, target):
+        remote(ref, ref, send_sem, recv_sem, {"batch": target}).start()
+
+    def arrive(ref, recv_sem):
+        pltpu.make_async_copy(ref, ref, recv_sem).wait()
+
+    for k in (3, 2, 1):
+        push(kvbuf.at[mine, z], kvz_send.at[0], kv_recv.at[z], index(x, zk[k], c))
+
     loads[0].wait()
     qbuf[x, :, :] = jnp.concatenate([qup_in[...], jnp.zeros((SLOT - QROWS, QR), BF16)], axis=0)
+    for target in (right, left):
+        push(qbuf.at[x], q_send.at[0], q_recv.at[x, 0], target)
     loads[1].wait()
     ql_own = ql_in[...].astype(F32)
     qlbuf[own, :, :] = jnp.concatenate(
         [ql_own[:, j * QC: (j + 1) * QC] for j in range(4)], axis=0
     ).astype(BF16)
-    loads[2].wait()
-
-    pl.semaphore_wait(barrier, ZS + YS - 1 + 6 + 2 + 1)
-
-    def remote(source, target, send_sem, recv_sem, device):
-        return pltpu.make_async_remote_copy(
-            src_ref=source, dst_ref=target, send_sem=send_sem, recv_sem=recv_sem,
-            device_id=device,
-        )
-
-    def push(ref, send_sem, recv_sem, target):
-        remote(ref, ref, send_sem, recv_sem, {"batch": target}).start()
-
-    def arrive(ref, recv_sem):
-        pltpu.make_async_copy(ref, ref, recv_sem).wait()
-
-    for target in (right, left):
-        push(qbuf.at[x], q_send.at[0], q_recv.at[x, 0], target)
-    for k in range(1, ZS):
-        push(kvbuf.at[mine, z], kvz_send.at[0], kv_recv.at[z], index(x, zk[k], c))
     for k in range(1, ZS):
         push(qlbuf.at[own], ql_send.at[0], ql_recv.at[own], index(x, zk[k], c))
     push(qlbuf.at[own], ql_send.at[0], ql_recv.at[own], sibling)

time: 46.1 us -> 45.7 us (level)
  Pallas kernels: 44.7 us -> 44.2 us
    pallas_call x1, Pallas kernels: 44.7 us -> 44.2 us  [shards(): pl.pallas_call(kernel, out_shape=jax.ShapeDtypeStruct((4, 448), F32), in_...]
where the time goes in v3:
time: 45.7 us; the launch traced here: 45.5 us
  Pallas kernels  44.2 us (97%)
  other arithmetic  1.29 us (3%)
    pallas_call x1, Pallas kernels, shards(): pl.pallas_call(kernel, out_shape=jax.ShapeDtypeStruct((4, 448), F32), in_...  44.2 us
    convert_element_type x1, other arithmetic, shards(): return pl.pallas_call(kernel, out_shape=jax.ShapeDtypeStruct((4, 448), F3...  1.29 us

profile of v3, /device:TPU:2, one launch (start us, length us, event | category | flops | bytes accessed | tf_op | source)
XLA Modules:
  0.0 45.5 jit_solution(7334655911811273520)
XLA Ops:
  0.0 44.2 %shard_map.91 = f32[4,448]{1,0:T(4,128)} custom-call(bf16[4,1536]{1,0:T(4,128)(2,1)} %ql_hbm.1, bf16[4,512]{1,0:T(4,128)(2,1)} %nl_hbm.1, bf16[4,64]{1,0:T(4,128)(2,1)} %nr_hbm.1, bf16[4,1024,512]{2,1,0:T(8,128)(2,1)} %lat_hbm.1, bf16[4,64,1024]{2,1,0:T(8,128)(2,1)} %bitcast.1, s32[4]{0:T(128)} %len_hbm.1, bf16[12,1536]{1,0:T(8,128)(2,1)} %qup_hbm.1, ...), custom_call_target="tpu_custom_call" | custom-call | flops 400000000 | bytes 5000000 | tf_op jit(solution)/shard_map/pallas_call | solution.py:380
  44.2 1.3 %convert_element_type.3 = bf16[4,448]{1,0:T(4,128)(2,1)} convert(f32[4,448]{1,0:T(4,128)} %shard_map.91) | non-fusion elementwise | flops 1792 | bytes 10752 | tf_op jit(solution)/shard_map/convert_element_type | solution.py:425

commit v4 on v3

--- a/solution.py
+++ b/solution.py
@@ -36,7 +36,7 @@
     ql_hbm, nl_hbm, nr_hbm, lat_hbm, rope_hbm, len_hbm, qup_hbm, kvup_hbm, outp_hbm, y_ref,
     ql_in, nl_in, nr_in, len_in, qup_in, outp_in, lat, rope,
     qbuf, qlbuf, qsend, qrecv, kvbuf, wbuf, sel, sel_out, vx, vh, ysend, yrecv,
-    in_sem, q_send, q_recv, ql_send, ql_recv, qx_send, qx_recv, kvz_send, kvb_send, kv_recv,
+    in_sem, q_send, q_recv, ql_send, ql_recv, qx_send, qx_recv, kvz_send, kvp_send, kvb_send, kv_recv,
     w_send, w_recv, vx_send, vx_recv, vh_send, vh_recv, y_send, y_recv,
 ):
     h = lax.axis_index("heads")
@@ -81,14 +81,15 @@
     for k in range(1, ZS):
         greet(index(x, zk[k], c))
         greet(index(x, zk[k], 1 - c))
-    greet(right)
-    greet(left)
+    for cc in (c, 1 - c):
+        greet(index(xr, z, cc))
+        greet(index(xl, z, cc))
     greet(sibling)
 
     for i in (2, 0, 1, 3, 4, 5, 6, 7, 8):
         loads[i].start()
     loads[2].wait()
-    pl.semaphore_wait(barrier, ZS + YS - 1 + 6 + 2 + 1)
+    pl.semaphore_wait(barrier, ZS + YS - 1 + 6 + 4 + 1)
 
     def remote(source, target, send_sem, recv_sem, device):
         return pltpu.make_async_remote_copy(
@@ -140,11 +141,19 @@
     arrive(qbuf.at[xr], q_recv.at[xr, 0])
     push(qbuf.at[xr, :, pl.ds(QR // 2, QR // 2)], q_send.at[0], q_recv.at[xr, 1], left)
 
-    for k in range(1, ZS):
+    def pair(block, half):
+        return kvbuf.at[block, pl.ds(2 * half, 2)]
+
+    def kv_pair_out(half):
+        for target in (right, left):
+            push(pair(mine, half), kvp_send.at[0], kv_recv.at[4 + x * 2 + half], target)
+
+    arrive(kvbuf.at[mine, zk[1]], kv_recv.at[zk[1]])
+    kv_pair_out(z // 2)
+    for k in range(2, ZS):
         arrive(kvbuf.at[mine, zk[k]], kv_recv.at[zk[k]])
-    for target in (right, left):
-        push(kvbuf.at[mine], kvb_send.at[0], kv_recv.at[4 + x], target)
-    push(kvbuf.at[mine], kvb_send.at[0], kv_recv.at[4 + x], sibling)
+    kv_pair_out(1 - z // 2)
+    push(kvbuf.at[mine], kvb_send.at[0], kv_recv.at[12 + x], sibling)
     for k in range(1, ZS):
         slot = zk[k] * 2 + c
         arrive(qlbuf.at[slot], ql_recv.at[slot])
@@ -154,12 +163,16 @@
     wbuf[mine, :, :] = jnp.concatenate([outp_in[...], jnp.zeros((2, OUT_K), BF16)], axis=0)
 
     from_left, from_right, from_far = xl * 2 + c, xr * 2 + c, xo * 2 + c
-    arrive(kvbuf.at[from_left], kv_recv.at[4 + xl])
-    push(kvbuf.at[from_left, pl.ds(0, 2)], kvb_send.at[0], kv_recv.at[12], right)
-    push(kvbuf.at[from_left], kvb_send.at[0], kv_recv.at[8 + xl], sibling)
-    arrive(kvbuf.at[from_right], kv_recv.at[4 + xr])
-    push(kvbuf.at[from_right, pl.ds(2, 2)], kvb_send.at[0], kv_recv.at[13], left)
-    push(kvbuf.at[from_right], kvb_send.at[0], kv_recv.at[8 + xr], sibling)
+    arrive(pair(from_left, 0), kv_recv.at[4 + xl * 2])
+    push(pair(from_left, 0), kvp_send.at[0], kv_recv.at[4 + xl * 2], right)
+    push(pair(from_left, 0), kvp_send.at[0], kv_recv.at[16], index(xr, z, 1 - c))
+    arrive(pair(from_right, 1), kv_recv.at[4 + xr * 2 + 1])
+    push(pair(from_right, 1), kvp_send.at[0], kv_recv.at[4 + xr * 2 + 1], left)
+    push(pair(from_right, 1), kvp_send.at[0], kv_recv.at[17], index(xl, z, 1 - c))
+    arrive(pair(from_left, 1), kv_recv.at[4 + xl * 2 + 1])
+    push(kvbuf.at[from_left], kvb_send.at[0], kv_recv.at[12 + xl], sibling)
+    arrive(pair(from_right, 0), kv_recv.at[4 + xr * 2])
+    push(kvbuf.at[from_right], kvb_send.at[0], kv_recv.at[12 + xr], sibling)
 
     for target in (right, left, sibling):
         push(wbuf.at[mine], w_send.at[0], w_recv.at[mine, 0], target)
@@ -191,10 +204,6 @@
         qsend.at[z * 2 + 1 - c], qrecv.at[own], qx_send.at[0], qx_recv.at[own], {"batch": sibling}
     ).start()
     qrecv[own, :, :] = qsend[own]
-
-    arrive(kvbuf.at[from_far, pl.ds(0, 2)], kv_recv.at[12])
-    arrive(kvbuf.at[from_far, pl.ds(2, 2)], kv_recv.at[13])
-    push(kvbuf.at[from_far], kvb_send.at[0], kv_recv.at[8 + xo], sibling)
 
     row8 = lax.broadcasted_iota(jnp.int32, (8, 1), 0)
     row_of = row8 % 4
@@ -241,10 +250,17 @@
         q_sel[:, 2 * NOPE: 2 * NOPE + ROPE] * cosine + q_sel[:, 2 * NOPE + ROPE:] * sine
     ).astype(BF16)
 
-    arrive(kvbuf.at[theirs], kv_recv.at[4 + x])
-    for xx in (xl, xr, xo):
+    loads[8].wait()
+    rope_scores = jnp.zeros((8, CACHE), F32)
+    for r in range(4):
+        rope_scores = jnp.where(row_of == r, dot_nn(query_rope, rope[r]), rope_scores)
+
+    for xx in (x, xl, xr):
         block = xx * 2 + 1 - c
-        arrive(kvbuf.at[block], kv_recv.at[8 + xx])
+        arrive(kvbuf.at[block], kv_recv.at[12 + xx])
+    for half in range(2):
+        arrive(pair(from_far, half), kv_recv.at[4 + xo * 2 + half])
+        arrive(pair(xo * 2 + 1 - c, half), kv_recv.at[16 + half])
 
     def kv_rows(xx):
         return jnp.concatenate(
@@ -256,12 +272,11 @@
     ).astype(BF16)
 
     loads[7].wait()
-    loads[8].wait()
     scale = (NOPE + ROPE) ** (-0.5)
     scores = jnp.zeros((8, CACHE), F32)
     for r in range(4):
-        of_row = dot_nt(query_abs, lat[r]) + dot_nn(query_rope, rope[r])
-        scores = jnp.where(row_of == r, of_row, scores)
+        scores = jnp.where(row_of == r, dot_nt(query_abs, lat[r]), scores)
+    scores = scores + rope_scores
     score_new = scale * (
         jnp.sum(query_abs.astype(F32) * nl8, axis=1, keepdims=True)
         + jnp.sum(query_rope.astype(F32) * key_new, axis=1, keepdims=True)
@@ -365,7 +380,8 @@
     y_ref[...] = dot_nn(summed, sel_out[...])[0:4]
 
     for ref, sem in (
-        (qbuf.at[0:3], q_send), (kvbuf.at[0, 0:3], kvz_send), (kvbuf.at[0:7], kvb_send),
+        (qbuf.at[0:3], q_send), (kvbuf.at[0, 0:3], kvz_send), (kvbuf.at[0:4], kvp_send),
+        (kvbuf.at[0:3], kvb_send),
         (qlbuf.at[0:7], ql_send), (qsend.at[0:7], qx_send), (wbuf.at[0:7], w_send),
         (vx.at[0:7], vx_send), (vh.at[0:7], vh_send), (ysend.at[0:3], y_send),
     ):
@@ -407,7 +423,7 @@
             dma((1,)), dma((XS, 2)),
             dma((1,)), dma((8,)),
             dma((1,)), dma((8,)),
-            dma((1,)), dma((1,)), dma((14,)),
+            dma((1,)), dma((1,)), dma((1,)), dma((18,)),
             dma((1,)), dma((8, 2)),
             dma((1,)), dma((2 * ZS,)),
             dma((1,)), dma((YS,)),

time: 45.7 us -> 45.4 us (level)
  no operation moved by 1% of the time
where the time goes in v4:
time: 45.4 us; the launch traced here: 45.2 us
  Pallas kernels  43.9 us (97%)
  other arithmetic  1.29 us (3%)
    pallas_call x1, Pallas kernels, shards(): pl.pallas_call(kernel, out_shape=jax.ShapeDtypeStruct((4, 448), F32), in_...  43.9 us
    convert_element_type x1, other arithmetic, shards(): return pl.pallas_call(kernel, out_shape=jax.ShapeDtypeStruct((4, 448), F3...  1.29 us

profile of v4, /device:TPU:2, one launch (start us, length us, event | category | flops | bytes accessed | tf_op | source)
XLA Modules:
  0.0 45.2 jit_solution(13931984727620765024)
XLA Ops:
  0.0 43.9 %shard_map.91 = f32[4,448]{1,0:T(4,128)} custom-call(bf16[4,1536]{1,0:T(4,128)(2,1)} %ql_hbm.1, bf16[4,512]{1,0:T(4,128)(2,1)} %nl_hbm.1, bf16[4,64]{1,0:T(4,128)(2,1)} %nr_hbm.1, bf16[4,1024,512]{2,1,0:T(8,128)(2,1)} %lat_hbm.1, bf16[4,64,1024]{2,1,0:T(8,128)(2,1)} %bitcast.1, s32[4]{0:T(128)} %len_hbm.1, bf16[12,1536]{1,0:T(8,128)(2,1)} %qup_hbm.1, ...), custom_call_target="tpu_custom_call" | custom-call | flops 400000000 | bytes 5000000 | tf_op jit(solution)/shard_map/pallas_call | solution.py:396
  43.9 1.3 %convert_element_type.3 = bf16[4,448]{1,0:T(4,128)(2,1)} convert(f32[4,448]{1,0:T(4,128)} %shard_map.91) | non-fusion elementwise | flops 1792 | bytes 10752 | tf_op jit(solution)/shard_map/convert_element_type | solution.py:441

commit v5 on v4

--- a/solution.py
+++ b/solution.py
@@ -121,7 +121,7 @@
 
     @pl.loop(0, 32)
     def _(t):
-        x_t = t % 4
+        x_t = (x + t % 4 + (t % 4) // 2 - 2 * ((t % 4) // 3)) % 4
         first_row = QROWS * ((x_t % 2) * 8 + (t // 8) * 2 + (t // 4) % 2)
         shape = (SLOT, 2 * NOPE + 2 * ROPE)
         within = lax.broadcasted_iota(jnp.int32, shape, 0)
@@ -177,17 +177,26 @@
     for target in (right, left, sibling):
         push(wbuf.at[mine], w_send.at[0], w_recv.at[mine, 0], target)
 
-    arrive(qbuf.at[xo, :, pl.ds(0, QR // 2)], q_recv.at[xo, 0])
-    arrive(qbuf.at[xo, :, pl.ds(QR // 2, QR // 2)], q_recv.at[xo, 1])
     for zz in range(ZS):
         slot = zz * 2 + 1 - c
         arrive(qlbuf.at[slot], ql_recv.at[slot])
     ql_rows = qlbuf[...].reshape(8 * SLOT, QC)
-    block_of = (lax.broadcasted_iota(jnp.int32, (8 * SLOT, XS * SLOT), 0) // 4) % 4
-    partial = jnp.zeros((8 * SLOT, XS * SLOT), F32)
-    for j in range(4):
-        columns = qbuf[:, :, j * QC: (j + 1) * QC].reshape(XS * SLOT, QC)
-        partial = jnp.where(block_of == j, dot_nt(ql_rows, columns), partial)
+
+    def partial_q(slots):
+        width = len(slots) * SLOT
+        block_of = (lax.broadcasted_iota(jnp.int32, (8 * SLOT, width), 0) // 4) % 4
+        total = jnp.zeros((8 * SLOT, width), F32)
+        for j in range(4):
+            columns = jnp.concatenate(
+                [qbuf[slot, :, j * QC: (j + 1) * QC] for slot in slots], axis=0
+            )
+            total = jnp.where(block_of == j, dot_nt(ql_rows, columns), total)
+        return total
+
+    near = partial_q([x, xr, xl])
+    arrive(qbuf.at[xo, :, pl.ds(0, QR // 2)], q_recv.at[xo, 0])
+    arrive(qbuf.at[xo, :, pl.ds(QR // 2, QR // 2)], q_recv.at[xo, 1])
+    partial = jnp.concatenate([near, partial_q([xo])], axis=1)
     partial = partial.reshape(8, SLOT, XS * SLOT)
     partial = partial[:, 0:8] + partial[:, 8:16]
     partial = jnp.concatenate([partial, partial], axis=2)
@@ -240,7 +249,9 @@
         pieces.append(piece + pltpu.roll(piece, 4, 0))
     q_all = jnp.concatenate(pieces, axis=1)
     lane_q = lax.broadcasted_iota(jnp.int32, (8, 512), 1)
-    q_all = jnp.where((lane_q % 64 < 32) == low, q_all, 0.0)
+    turn = lane_q % 64 // 16
+    x_of = (x + turn + turn // 2 - 2 * (turn // 3)) % 4
+    q_all = jnp.where((x_of < 2) == low, q_all, 0.0)
     q_hi = q_all.astype(BF16)
     q_lo = (q_all - q_hi.astype(F32)).astype(BF16)
     selection = sel[...]
@@ -349,19 +360,21 @@
         block = xx * 2 + 1 - c
         arrive(wbuf.at[block], w_recv.at[block, 0])
 
-    for i in (1, 7, 2, 6, 3, 5, 4):
-        other = (y + i) % YS
-        arrive(vh.at[other], vh_recv.at[other])
-
     row32 = lax.broadcasted_iota(jnp.int32, (32, 128), 0)
     is_low = (row32 % 8) < 4
     zero = jnp.zeros((32, 128), BF16)
-    chunks = []
-    for hh in range(2 * YS):
-        block = vh[hh % YS, hh // YS * 32: hh // YS * 32 + 32]
-        chunks.append(jnp.where(is_low, block, zero))
-        chunks.append(jnp.where(is_low, zero, block))
-    y_all = dot_nt(jnp.concatenate(chunks, axis=1), wbuf[...].reshape(8 * SLOT, OUT_K))
+    y_all = jnp.zeros((32, 128), F32)
+    for i in (0, 1, 7, 2, 6, 3, 5, 4):
+        other = (y + i) % YS
+        if i:
+            arrive(vh.at[other], vh_recv.at[other])
+        for half in range(2):
+            block = vh[other, half * 32: half * 32 + 32]
+            block = jnp.concatenate(
+                [jnp.where(is_low, block, zero), jnp.where(is_low, zero, block)], axis=1
+            )
+            columns = pl.ds(pl.multiple_of((half * YS + other) * 256, 256), 256)
+            y_all = y_all + dot_nt(block, wbuf[:, :, columns].reshape(8 * SLOT, 256))
     ysend[...] = y_all.reshape(ZS, 8, 128)
 
     for k in range(1, ZS):

time: 45.4 us -> 45.3 us (level)
  no operation moved by 1% of the time
where the time goes in v5:
time: 45.3 us; the launch traced here: 45.1 us
  Pallas kernels  43.8 us (97%)
  other arithmetic  1.29 us (3%)
    pallas_call x1, Pallas kernels, shards(): pl.pallas_call(kernel, out_shape=jax.ShapeDtypeStruct((4, 448), F32), in_...  43.8 us
    convert_element_type x1, other arithmetic, shards(): return pl.pallas_call(kernel, out_shape=jax.ShapeDtypeStruct((4, 448), F3...  1.29 us

profile of v5, /device:TPU:2, one launch (start us, length us, event | category | flops | bytes accessed | tf_op | source)
XLA Modules:
  0.0 45.1 jit_solution(8403129495534298862)
XLA Ops:
  0.0 43.8 %shard_map.91 = f32[4,448]{1,0:T(4,128)} custom-call(bf16[4,1536]{1,0:T(4,128)(2,1)} %ql_hbm.1, bf16[4,512]{1,0:T(4,128)(2,1)} %nl_hbm.1, bf16[4,64]{1,0:T(4,128)(2,1)} %nr_hbm.1, bf16[4,1024,512]{2,1,0:T(8,128)(2,1)} %lat_hbm.1, bf16[4,64,1024]{2,1,0:T(8,128)(2,1)} %bitcast.1, s32[4]{0:T(128)} %len_hbm.1, bf16[12,1536]{1,0:T(8,128)(2,1)} %qup_hbm.1, ...), custom_call_target="tpu_custom_call" | custom-call | flops 400000000 | bytes 5000000 | tf_op jit(solution)/shard_map/pallas_call | solution.py:409
  43.8 1.3 %convert_element_type.3 = bf16[4,448]{1,0:T(4,128)(2,1)} convert(f32[4,448]{1,0:T(4,128)} %shard_map.91) | non-fusion elementwise | flops 1792 | bytes 10752 | tf_op jit(solution)/shard_map/convert_element_type | solution.py:454

commit v6 on v5

--- a/solution.py
+++ b/solution.py
@@ -162,6 +162,9 @@
     loads[6].wait()
     wbuf[mine, :, :] = jnp.concatenate([outp_in[...], jnp.zeros((2, OUT_K), BF16)], axis=0)
 
+    for target in (right, left, sibling):
+        push(wbuf.at[mine], w_send.at[0], w_recv.at[mine, 0], target)
+
     from_left, from_right, from_far = xl * 2 + c, xr * 2 + c, xo * 2 + c
     arrive(pair(from_left, 0), kv_recv.at[4 + xl * 2])
     push(pair(from_left, 0), kvp_send.at[0], kv_recv.at[4 + xl * 2], right)
@@ -174,9 +177,6 @@
     arrive(pair(from_right, 0), kv_recv.at[4 + xr * 2])
     push(kvbuf.at[from_right], kvb_send.at[0], kv_recv.at[12 + xr], sibling)
 
-    for target in (right, left, sibling):
-        push(wbuf.at[mine], w_send.at[0], w_recv.at[mine, 0], target)
-
     for zz in range(ZS):
         slot = zz * 2 + 1 - c
         arrive(qlbuf.at[slot], ql_recv.at[slot])
@@ -213,6 +213,18 @@
         qsend.at[z * 2 + 1 - c], qrecv.at[own], qx_send.at[0], qx_recv.at[own], {"batch": sibling}
     ).start()
     qrecv[own, :, :] = qsend[own]
+
+    arrive(wbuf.at[from_left], w_recv.at[from_left, 0])
+    push(
+        wbuf.at[from_left, :, pl.ds(0, OUT_K // 2)], w_send.at[0], w_recv.at[from_left, 0], right
+    )
+    push(wbuf.at[from_left], w_send.at[0], w_recv.at[from_left, 0], sibling)
+    arrive(wbuf.at[from_right], w_recv.at[from_right, 0])
+    push(
+        wbuf.at[from_right, :, pl.ds(OUT_K // 2, OUT_K // 2)], w_send.at[0],
+        w_recv.at[from_right, 1], left,
+    )
+    push(wbuf.at[from_right], w_send.at[0], w_recv.at[from_right, 0], sibling)
 
     row8 = lax.broadcasted_iota(jnp.int32, (8, 1), 0)
     row_of = row8 % 4
@@ -288,6 +300,10 @@
     for r in range(4):
         scores = jnp.where(row_of == r, dot_nt(query_abs, lat[r]), scores)
     scores = scores + rope_scores
+    arrive(wbuf.at[from_far, :, pl.ds(0, OUT_K // 2)], w_recv.at[from_far, 0])
+    arrive(wbuf.at[from_far, :, pl.ds(OUT_K // 2, OUT_K // 2)], w_recv.at[from_far, 1])
+    push(wbuf.at[from_far], w_send.at[0], w_recv.at[from_far, 0], sibling)
+
     score_new = scale * (
         jnp.sum(query_abs.astype(F32) * nl8, axis=1, keepdims=True)
         + jnp.sum(query_rope.astype(F32) * key_new, axis=1, keepdims=True)
@@ -319,18 +335,6 @@
     for k in range(1, ZS):
         vx_push(h, k)
 
-    arrive(wbuf.at[from_left], w_recv.at[from_left, 0])
-    push(
-        wbuf.at[from_left, :, pl.ds(0, OUT_K // 2)], w_send.at[0], w_recv.at[from_left, 0], right
-    )
-    push(wbuf.at[from_left], w_send.at[0], w_recv.at[from_left, 0], sibling)
-    arrive(wbuf.at[from_right], w_recv.at[from_right, 0])
-    push(
-        wbuf.at[from_right, :, pl.ds(OUT_K // 2, OUT_K // 2)], w_send.at[0],
-        w_recv.at[from_right, 1], left,
-    )
-    push(wbuf.at[from_right], w_send.at[0], w_recv.at[from_right, 0], sibling)
-
     for k in range(1, ZS):
         arrive(vx.at[up * ZS + zk[k]], vx_recv.at[up * ZS + zk[k]])
     for k in range(ZS):
@@ -343,10 +347,6 @@
             vh.at[y], vh.at[y], vh_send.at[0], vh_recv.at[y],
             {"heads": up * YS + (y + i) % YS},
         ).start()
-
-    arrive(wbuf.at[from_far, :, pl.ds(0, OUT_K // 2)], w_recv.at[from_far, 0])
-    arrive(wbuf.at[from_far, :, pl.ds(OUT_K // 2, OUT_K // 2)], w_recv.at[from_far, 1])
-    push(wbuf.at[from_far], w_send.at[0], w_recv.at[from_far, 0], sibling)
 
     @pl.loop(0, 32)
     def _(t):

time: 45.3 us -> 46 us (1.015)
  Pallas kernels: 43.8 us -> 44.5 us
    pallas_call x1, Pallas kernels: 43.8 us -> 44.5 us  [shards(): pl.pallas_call(kernel, out_shape=jax.ShapeDtypeStruct((4, 448), F32), in_...]
where the time goes in v6:
time: 46 us; the launch traced here: 45.8 us
  Pallas kernels  44.5 us (97%)
  other arithmetic  1.29 us (3%)
    pallas_call x1, Pallas kernels, shards(): pl.pallas_call(kernel, out_shape=jax.ShapeDtypeStruct((4, 448), F32), in_...  44.5 us
    convert_element_type x1, other arithmetic, shards(): return pl.pallas_call(kernel, out_shape=jax.ShapeDtypeStruct((4, 448), F3...  1.29 us

profile of v6, /device:TPU:2, one launch (start us, length us, event | category | flops | bytes accessed | tf_op | source)
XLA Modules:
  0.0 45.8 jit_solution(15650726534773676158)
XLA Ops:
  0.0 44.5 %shard_map.91 = f32[4,448]{1,0:T(4,128)} custom-call(bf16[4,1536]{1,0:T(4,128)(2,1)} %ql_hbm.1, bf16[4,512]{1,0:T(4,128)(2,1)} %nl_hbm.1, bf16[4,64]{1,0:T(4,128)(2,1)} %nr_hbm.1, bf16[4,1024,512]{2,1,0:T(8,128)(2,1)} %lat_hbm.1, bf16[4,64,1024]{2,1,0:T(8,128)(2,1)} %bitcast.1, s32[4]{0:T(128)} %len_hbm.1, bf16[12,1536]{1,0:T(8,128)(2,1)} %qup_hbm.1, ...), custom_call_target="tpu_custom_call" | custom-call | flops 400000000 | bytes 5000000 | tf_op jit(solution)/shard_map/pallas_call | solution.py:409
  44.5 1.3 %convert_element_type.3 = bf16[4,448]{1,0:T(4,128)(2,1)} convert(f32[4,448]{1,0:T(4,128)} %shard_map.91) | non-fusion elementwise | flops 1792 | bytes 10752 | tf_op jit(solution)/shard_map/convert_element_type | solution.py:454

commit v7 on v5

--- a/solution.py
+++ b/solution.py
@@ -262,9 +262,11 @@
     ).astype(BF16)
 
     loads[8].wait()
-    rope_scores = jnp.zeros((8, CACHE), F32)
-    for r in range(4):
-        rope_scores = jnp.where(row_of == r, dot_nn(query_rope, rope[r]), rope_scores)
+
+    def rope_row(r, scores):
+        return jnp.where(row_of == r, dot_nn(query_rope, rope[r]), scores)
+
+    rope_scores = lax.fori_loop(0, 4, rope_row, jnp.zeros((8, CACHE), F32))
 
     for xx in (x, xl, xr):
         block = xx * 2 + 1 - c
@@ -284,10 +286,10 @@
 
     loads[7].wait()
     scale = (NOPE + ROPE) ** (-0.5)
-    scores = jnp.zeros((8, CACHE), F32)
-    for r in range(4):
-        scores = jnp.where(row_of == r, dot_nt(query_abs, lat[r]), scores)
-    scores = scores + rope_scores
+    def score_row(r, scores):
+        return jnp.where(row_of == r, scores + dot_nt(query_abs, lat[r]), scores)
+
+    scores = lax.fori_loop(0, 4, score_row, rope_scores)
     score_new = scale * (
         jnp.sum(query_abs.astype(F32) * nl8, axis=1, keepdims=True)
         + jnp.sum(query_rope.astype(F32) * key_new, axis=1, keepdims=True)
@@ -300,9 +302,10 @@
     denom = jnp.sum(old, axis=1, keepdims=True) + new
     probs = (old / denom).astype(BF16)
     prob_new = (new / denom).astype(BF16).astype(F32)
-    context = jnp.zeros((8, KVR), F32)
-    for r in range(4):
-        context = jnp.where(row_of == r, dot_nn(probs, lat[r]), context)
+    def context_row(r, context):
+        return jnp.where(row_of == r, dot_nn(probs, lat[r]), context)
+
+    context = lax.fori_loop(0, 4, context_row, jnp.zeros((8, KVR), F32))
     context = (context + prob_new * nl8).astype(BF16)
     value = jnp.where(low, dot_nt(context, kv_rows(1)), dot_nt(context, kv_rows(3)))
     z_of_8 = up * ZS + z

time: 45.3 us -> 46.3 us (1.022)
  Pallas kernels: 43.8 us -> 44.7 us
    pallas_call x1, Pallas kernels: 43.8 us -> 44.7 us  [shards(): pl.pallas_call(kernel, out_shape=jax.ShapeDtypeStruct((4, 448), F32), in_...]
where the time goes in v7:
time: 46.3 us; the launch traced here: 46 us
  Pallas kernels  44.7 us (97%)
  other arithmetic  1.29 us (3%)
    pallas_call x1, Pallas kernels, shards(): pl.pallas_call(kernel, out_shape=jax.ShapeDtypeStruct((4, 448), F32), in_...  44.7 us
    convert_element_type x1, other arithmetic, shards(): return pl.pallas_call(kernel, out_shape=jax.ShapeDtypeStruct((4, 448), F3...  1.29 us

profile of v7, /device:TPU:2, one launch (start us, length us, event | category | flops | bytes accessed | tf_op | source)
XLA Modules:
  0.0 46.0 jit_solution(17177924035543751138)
XLA Ops:
  0.0 44.7 %shard_map.91 = f32[4,448]{1,0:T(4,128)} custom-call(bf16[4,1536]{1,0:T(4,128)(2,1)} %ql_hbm.1, bf16[4,512]{1,0:T(4,128)(2,1)} %nl_hbm.1, bf16[4,64]{1,0:T(4,128)(2,1)} %nr_hbm.1, bf16[4,1024,512]{2,1,0:T(8,128)(2,1)} %lat_hbm.1, bf16[4,64,1024]{2,1,0:T(8,128)(2,1)} %bitcast.1, s32[4]{0:T(128)} %len_hbm.1, bf16[12,1536]{1,0:T(8,128)(2,1)} %qup_hbm.1, ...), custom_call_target="tpu_custom_call" | custom-call | flops 400000000 | bytes 5000000 | tf_op jit(solution)/shard_map/pallas_call | solution.py:412
  44.7 1.3 %convert_element_type.3 = bf16[4,448]{1,0:T(4,128)(2,1)} convert(f32[4,448]{1,0:T(4,128)} %shard_map.91) | non-fusion elementwise | flops 1792 | bytes 10752 | tf_op jit(solution)/shard_map/convert_element_type | solution.py:457

commit v8 on v5

--- a/solution.py
+++ b/solution.py
@@ -306,18 +306,19 @@
     context = (context + prob_new * nl8).astype(BF16)
     value = jnp.where(low, dot_nt(context, kv_rows(1)), dot_nt(context, kv_rows(3)))
     z_of_8 = up * ZS + z
-    vx[z_of_8, :, :] = value.astype(BF16).astype(F32)
-
-    def vx_push(heads, k):
+    first_at = z_of_8 * (1 - c) + y * c
+    second_at = y * (1 - c) + z_of_8 * c
+
+    def ring_peer(steps_z, steps_y):
+        to_z, to_y = (z_of_8 + steps_z) % 8, (y + steps_y) % YS
+        return {"heads": to_z // ZS * YS + to_y, "batch": index(x, to_z % ZS, c)}
+
+    vx[first_at, :, :] = value.astype(BF16).astype(F32)
+    for i in (4, 3, 5, 2, 6, 1, 7):
         remote(
-            vx.at[z_of_8], vx.at[z_of_8], vx_send.at[0], vx_recv.at[z_of_8],
-            {"heads": heads, "batch": index(x, zk[k], c)},
+            vx.at[first_at], vx.at[first_at], vx_send.at[0], vx_recv.at[first_at],
+            ring_peer(i * (1 - c), i * c),
         ).start()
-
-    for k in range(ZS):
-        vx_push(across, k)
-    for k in range(1, ZS):
-        vx_push(h, k)
 
     arrive(wbuf.at[from_left], w_recv.at[from_left, 0])
     push(
@@ -331,17 +332,15 @@
     )
     push(wbuf.at[from_right], w_send.at[0], w_recv.at[from_right, 0], sibling)
 
-    for k in range(1, ZS):
-        arrive(vx.at[up * ZS + zk[k]], vx_recv.at[up * ZS + zk[k]])
-    for k in range(ZS):
-        slot = (1 - up) * ZS + zk[k]
+    for i in (1, 7, 2, 6, 3, 5, 4):
+        slot = (first_at + i) % 8
         arrive(vx.at[slot], vx_recv.at[slot])
-    vh[y, :, :] = vx[...].reshape(64, 128).astype(BF16)
+    vh[second_at, :, :] = vx[...].reshape(64, 128).astype(BF16)
 
     for i in (4, 3, 5, 2, 6, 1, 7):
         remote(
-            vh.at[y], vh.at[y], vh_send.at[0], vh_recv.at[y],
-            {"heads": up * YS + (y + i) % YS},
+            vh.at[second_at], vh.at[second_at], vh_send.at[0], vh_recv.at[second_at],
+            ring_peer(i * c, i * (1 - c)),
         ).start()
 
     arrive(wbuf.at[from_far, :, pl.ds(0, OUT_K // 2)], w_recv.at[from_far, 0])
@@ -363,19 +362,40 @@
     row32 = lax.broadcasted_iota(jnp.int32, (32, 128), 0)
     is_low = (row32 % 8) < 4
     zero = jnp.zeros((32, 128), BF16)
-    y_all = jnp.zeros((32, 128), F32)
-    for i in (0, 1, 7, 2, 6, 3, 5, 4):
-        other = (y + i) % YS
-        if i:
+
+    def by_head(block):
+        return jnp.concatenate(
+            [jnp.where(is_low, block, zero), jnp.where(is_low, zero, block)], axis=1
+        )
+
+    def out_rows(half, at_y):
+        columns = pl.ds(pl.multiple_of((half * YS + at_y) * 256, 256), 256)
+        return wbuf[:, :, columns].reshape(8 * SLOT, 256)
+
+    @pl.when(c == 0)
+    def _():
+        y_all = jnp.zeros((32, 128), F32)
+        for i in (0, 1, 7, 2, 6, 3, 5, 4):
+            other = (y + i) % YS
+            if i:
+                arrive(vh.at[other], vh_recv.at[other])
+            for half in range(2):
+                block = vh[other, half * 32: half * 32 + 32]
+                y_all = y_all + dot_nt(by_head(block), out_rows(half, other))
+        ysend[...] = y_all.reshape(ZS, 8, 128)
+
+    @pl.when(c == 1)
+    def _():
+        for i in (1, 7, 2, 6, 3, 5, 4):
+            other = (z_of_8 + i) % 8
             arrive(vh.at[other], vh_recv.at[other])
+        y_all = jnp.zeros((32, 128), F32)
         for half in range(2):
-            block = vh[other, half * 32: half * 32 + 32]
-            block = jnp.concatenate(
-                [jnp.where(is_low, block, zero), jnp.where(is_low, zero, block)], axis=1
-            )
-            columns = pl.ds(pl.multiple_of((half * YS + other) * 256, 256), 256)
-            y_all = y_all + dot_nt(block, wbuf[:, :, columns].reshape(8 * SLOT, 256))
-    ysend[...] = y_all.reshape(ZS, 8, 128)
+            blocks = vh[half * ZS: half * ZS + ZS].astype(F32).reshape(ZS, YS, 8, 128)
+            for at_y in range(YS):
+                block = blocks[:, at_y].reshape(32, 128).astype(BF16)
+                y_all = y_all + dot_nt(by_head(block), out_rows(half, at_y))
+        ysend[...] = y_all.reshape(ZS, 8, 128)
 
     for k in range(1, ZS):
         remote(

time: 45.3 us -> 45 us (level)
  the two profiles are of different devices: /device:TPU:2 before, /device:TPU:8 now
where the time goes in v8:
time: 45 us; the launch traced here: 44.8 us
  Pallas kernels  43.5 us (97%)
  other arithmetic  1.29 us (3%)
    pallas_call x1, Pallas kernels, shards(): pl.pallas_call(kernel, out_shape=jax.ShapeDtypeStruct((4, 448), F32), in_...  43.5 us
    convert_element_type x1, other arithmetic, shards(): return pl.pallas_call(kernel, out_shape=jax.ShapeDtypeStruct((4, 448), F3...  1.29 us

profile of v8, /device:TPU:8, one launch (start us, length us, event | category | flops | bytes accessed | tf_op | source)
XLA Modules:
  0.0 44.8 jit_solution(8415156979025237390)
XLA Ops:
  0.0 43.5 %shard_map.91 = f32[4,448]{1,0:T(4,128)} custom-call(bf16[4,1536]{1,0:T(4,128)(2,1)} %ql_hbm.1, bf16[4,512]{1,0:T(4,128)(2,1)} %nl_hbm.1, bf16[4,64]{1,0:T(4,128)(2,1)} %nr_hbm.1, bf16[4,1024,512]{2,1,0:T(8,128)(2,1)} %lat_hbm.1, bf16[4,64,1024]{2,1,0:T(8,128)(2,1)} %bitcast.1, s32[4]{0:T(128)} %len_hbm.1, bf16[12,1536]{1,0:T(8,128)(2,1)} %qup_hbm.1, ...), custom_call_target="tpu_custom_call" | custom-call | flops 400000000 | bytes 5000000 | tf_op jit(solution)/shard_map/pallas_call | solution.py:429
  43.5 1.3 %convert_element_type.3 = bf16[4,448]{1,0:T(4,128)(2,1)} convert(f32[4,448]{1,0:T(4,128)} %shard_map.91) | non-fusion elementwise | flops 1792 | bytes 10752 | tf_op jit(solution)/shard_map/convert_element_type | solution.py:474

commit v9 on v8

--- a/solution.py
+++ b/solution.py
@@ -306,8 +306,8 @@
     context = (context + prob_new * nl8).astype(BF16)
     value = jnp.where(low, dot_nt(context, kv_rows(1)), dot_nt(context, kv_rows(3)))
     z_of_8 = up * ZS + z
-    first_at = z_of_8 * (1 - c) + y * c
-    second_at = y * (1 - c) + z_of_8 * c
+    first_at = z_of_8 * c + y * (1 - c)
+    second_at = y * c + z_of_8 * (1 - c)
 
     def ring_peer(steps_z, steps_y):
         to_z, to_y = (z_of_8 + steps_z) % 8, (y + steps_y) % YS
@@ -317,7 +317,7 @@
     for i in (4, 3, 5, 2, 6, 1, 7):
         remote(
             vx.at[first_at], vx.at[first_at], vx_send.at[0], vx_recv.at[first_at],
-            ring_peer(i * (1 - c), i * c),
+            ring_peer(i * c, i * (1 - c)),
         ).start()
 
     arrive(wbuf.at[from_left], w_recv.at[from_left, 0])
@@ -340,7 +340,7 @@
     for i in (4, 3, 5, 2, 6, 1, 7):
         remote(
             vh.at[second_at], vh.at[second_at], vh_send.at[0], vh_recv.at[second_at],
-            ring_peer(i * c, i * (1 - c)),
+            ring_peer(i * (1 - c), i * c),
         ).start()
 
     arrive(wbuf.at[from_far, :, pl.ds(0, OUT_K // 2)], w_recv.at[from_far, 0])
@@ -372,7 +372,7 @@
         columns = pl.ds(pl.multiple_of((half * YS + at_y) * 256, 256), 256)
         return wbuf[:, :, columns].reshape(8 * SLOT, 256)
 
-    @pl.when(c == 0)
+    @pl.when(c == 1)
     def _():
         y_all = jnp.zeros((32, 128), F32)
         for i in (0, 1, 7, 2, 6, 3, 5, 4):
@@ -384,7 +384,7 @@
                 y_all = y_all + dot_nt(by_head(block), out_rows(half, other))
         ysend[...] = y_all.reshape(ZS, 8, 128)
 
-    @pl.when(c == 1)
+    @pl.when(c == 0)
     def _():
         for i in (1, 7, 2, 6, 3, 5, 4):
             other = (z_of_8 + i) % 8

time: 45 us -> 45.5 us (1.011)
  the two profiles are of different devices: /device:TPU:8 before, /device:TPU:2 now
where the time goes in v9:
time: 45.5 us; the launch traced here: 45.2 us
  Pallas kernels  43.9 us (96%)
  other arithmetic  1.29 us (3%)
    pallas_call x1, Pallas kernels, shards(): pl.pallas_call(kernel, out_shape=jax.ShapeDtypeStruct((4, 448), F32), in_...  43.9 us
    convert_element_type x1, other arithmetic, shards(): return pl.pallas_call(kernel, out_shape=jax.ShapeDtypeStruct((4, 448), F3...  1.29 us

profile of v9, /device:TPU:2, one launch (start us, length us, event | category | flops | bytes accessed | tf_op | source)
XLA Modules:
  0.0 45.2 jit_solution(10287191737254315949)
XLA Ops:
  0.0 43.9 %shard_map.91 = f32[4,448]{1,0:T(4,128)} custom-call(bf16[4,1536]{1,0:T(4,128)(2,1)} %ql_hbm.1, bf16[4,512]{1,0:T(4,128)(2,1)} %nl_hbm.1, bf16[4,64]{1,0:T(4,128)(2,1)} %nr_hbm.1, bf16[4,1024,512]{2,1,0:T(8,128)(2,1)} %lat_hbm.1, bf16[4,64,1024]{2,1,0:T(8,128)(2,1)} %bitcast.1, s32[4]{0:T(128)} %len_hbm.1, bf16[12,1536]{1,0:T(8,128)(2,1)} %qup_hbm.1, ...), custom_call_target="tpu_custom_call" | custom-call | flops 400000000 | bytes 5000000 | tf_op jit(solution)/shard_map/pallas_call | solution.py:429
  43.9 1.3 %convert_element_type.3 = bf16[4,448]{1,0:T(4,128)(2,1)} convert(f32[4,448]{1,0:T(4,128)} %shard_map.91) | non-fusion elementwise | flops 1792 | bytes 10752 | tf_op jit(solution)/shard_map/convert_element_type | solution.py:474

commit v10 on v8

--- a/solution.py
+++ b/solution.py
@@ -253,9 +253,11 @@
     x_of = (x + turn + turn // 2 - 2 * (turn // 3)) % 4
     q_all = jnp.where((x_of < 2) == low, q_all, 0.0)
     q_hi = q_all.astype(BF16)
-    q_lo = (q_all - q_hi.astype(F32)).astype(BF16)
+    q_lo = q_all - q_hi.astype(F32)
     selection = sel[...]
-    q_sel = dot_nn(q_hi, selection) + dot_nn(q_lo, selection)
+    q_both = jnp.concatenate([q_hi.astype(F32), q_lo], axis=0).astype(BF16)
+    q_both = dot_nn(q_both, selection)
+    q_sel = q_both[0:8] + q_both[8:16]
     q_nope = q_sel[:, 0: 2 * NOPE].astype(BF16)
     query_rope = (
         q_sel[:, 2 * NOPE: 2 * NOPE + ROPE] * cosine + q_sel[:, 2 * NOPE + ROPE:] * sine
@@ -266,12 +268,20 @@
     for r in range(4):
         rope_scores = jnp.where(row_of == r, dot_nn(query_rope, rope[r]), rope_scores)
 
-    for xx in (x, xl, xr):
-        block = xx * 2 + 1 - c
-        arrive(kvbuf.at[block], kv_recv.at[12 + xx])
-    for half in range(2):
-        arrive(pair(from_far, half), kv_recv.at[4 + xo * 2 + half])
-        arrive(pair(xo * 2 + 1 - c, half), kv_recv.at[16 + half])
+    def blocks_for(parity):
+        @pl.when(x % 2 == parity)
+        def _():
+            arrive(kvbuf.at[x * 2 + 1 - c], kv_recv.at[12 + x])
+            for half in range(2):
+                arrive(pair(from_far, half), kv_recv.at[4 + xo * 2 + half])
+                arrive(pair(xo * 2 + 1 - c, half), kv_recv.at[16 + half])
+
+        @pl.when(x % 2 != parity)
+        def _():
+            for xx in (xl, xr):
+                arrive(kvbuf.at[xx * 2 + 1 - c], kv_recv.at[12 + xx])
+
+    blocks_for(0)
 
     def kv_rows(xx):
         return jnp.concatenate(
@@ -304,6 +314,7 @@
     for r in range(4):
         context = jnp.where(row_of == r, dot_nn(probs, lat[r]), context)
     context = (context + prob_new * nl8).astype(BF16)
+    blocks_for(1)
     value = jnp.where(low, dot_nt(context, kv_rows(1)), dot_nt(context, kv_rows(3)))
     z_of_8 = up * ZS + z
     first_at = z_of_8 * (1 - c) + y * c

time: 45 us -> 45 us (level)
  no operation moved by 1% of the time
where the time goes in v10:
time: 45 us; the launch traced here: 44.8 us
  Pallas kernels  43.5 us (97%)
  other arithmetic  1.29 us (3%)
    pallas_call x1, Pallas kernels, shards(): pl.pallas_call(kernel, out_shape=jax.ShapeDtypeStruct((4, 448), F32), in_...  43.5 us
    convert_element_type x1, other arithmetic, shards(): return pl.pallas_call(kernel, out_shape=jax.ShapeDtypeStruct((4, 448), F3...  1.29 us

profile of v10, /device:TPU:8, one launch (start us, length us, event | category | flops | bytes accessed | tf_op | source)
XLA Modules:
  0.0 44.8 jit_solution(14292741976463406544)
XLA Ops:
  0.0 43.5 %shard_map.91 = f32[4,448]{1,0:T(4,128)} custom-call(bf16[4,1536]{1,0:T(4,128)(2,1)} %ql_hbm.1, bf16[4,512]{1,0:T(4,128)(2,1)} %nl_hbm.1, bf16[4,64]{1,0:T(4,128)(2,1)} %nr_hbm.1, bf16[4,1024,512]{2,1,0:T(8,128)(2,1)} %lat_hbm.1, bf16[4,64,1024]{2,1,0:T(8,128)(2,1)} %bitcast.1, s32[4]{0:T(128)} %len_hbm.1, bf16[12,1536]{1,0:T(8,128)(2,1)} %qup_hbm.1, ...), custom_call_target="tpu_custom_call" | custom-call | flops 400000000 | bytes 5000000 | tf_op jit(solution)/shard_map/pallas_call | solution.py:440
  43.5 1.3 %convert_element_type.3 = bf16[4,448]{1,0:T(4,128)(2,1)} convert(f32[4,448]{1,0:T(4,128)} %shard_map.91) | non-fusion elementwise | flops 1792 | bytes 10752 | tf_op jit(solution)/shard_map/convert_element_type | solution.py:485

commit v11 on v10

--- a/solution.py
+++ b/solution.py
@@ -202,7 +202,7 @@
     partial = jnp.concatenate([partial, partial], axis=2)
     lane_of = lax.broadcasted_iota(jnp.int32, (8, 8, 128), 2)
     qsend[...] = jnp.where(lane_of // 64 == c, partial, 0.0)
-    for k in range(1, ZS):
+    for k in (3, 2, 1):
         for cc in (c, 1 - c):
             slot = zk[k] * 2 + cc
             remote(
@@ -408,7 +408,7 @@
                 y_all = y_all + dot_nt(by_head(block), out_rows(half, at_y))
         ysend[...] = y_all.reshape(ZS, 8, 128)
 
-    for k in range(1, ZS):
+    for k in (3, 2, 1):
         remote(
             ysend.at[zk[k]], yrecv.at[z], y_send.at[0], y_recv.at[z],
             {"batch": index(x, zk[k], c)},

time: 45 us -> 44.7 us (level)
  no operation moved by 1% of the time
where the time goes in v11:
time: 44.7 us; the launch traced here: 44.5 us
  Pallas kernels  43.2 us (97%)
  other arithmetic  1.29 us (3%)
    pallas_call x1, Pallas kernels, shards(): pl.pallas_call(kernel, out_shape=jax.ShapeDtypeStruct((4, 448), F32), in_...  43.2 us
    convert_element_type x1, other arithmetic, shards(): return pl.pallas_call(kernel, out_shape=jax.ShapeDtypeStruct((4, 448), F3...  1.29 us

profile of v11, /device:TPU:8, one launch (start us, length us, event | category | flops | bytes accessed | tf_op | source)
XLA Modules:
  0.0 44.5 jit_solution(13491555501793230503)
XLA Ops:
  0.0 43.2 %shard_map.91 = f32[4,448]{1,0:T(4,128)} custom-call(bf16[4,1536]{1,0:T(4,128)(2,1)} %ql_hbm.1, bf16[4,512]{1,0:T(4,128)(2,1)} %nl_hbm.1, bf16[4,64]{1,0:T(4,128)(2,1)} %nr_hbm.1, bf16[4,1024,512]{2,1,0:T(8,128)(2,1)} %lat_hbm.1, bf16[4,64,1024]{2,1,0:T(8,128)(2,1)} %bitcast.1, s32[4]{0:T(128)} %len_hbm.1, bf16[12,1536]{1,0:T(8,128)(2,1)} %qup_hbm.1, ...), custom_call_target="tpu_custom_call" | custom-call | flops 400000000 | bytes 5000000 | tf_op jit(solution)/shard_map/pallas_call | solution.py:440
  43.2 1.3 %convert_element_type.3 = bf16[4,448]{1,0:T(4,128)(2,1)} convert(f32[4,448]{1,0:T(4,128)} %shard_map.91) | non-fusion elementwise | flops 1792 | bytes 10752 | tf_op jit(solution)/shard_map/convert_element_type | solution.py:485

commit v12 on v11

--- a/solution.py
+++ b/solution.py
@@ -78,7 +78,7 @@
     def _(i):
         pl.semaphore_signal(barrier, inc=1, device_id={"heads": up * YS + (y + i) % YS})
 
-    for k in range(1, ZS):
+    for k in (3, 2, 1):
         greet(index(x, zk[k], c))
         greet(index(x, zk[k], 1 - c))
     for cc in (c, 1 - c):
@@ -115,7 +115,7 @@
     qlbuf[own, :, :] = jnp.concatenate(
         [ql_own[:, j * QC: (j + 1) * QC] for j in range(4)], axis=0
     ).astype(BF16)
-    for k in range(1, ZS):
+    for k in (3, 2, 1):
         push(qlbuf.at[own], ql_send.at[0], ql_recv.at[own], index(x, zk[k], c))
     push(qlbuf.at[own], ql_send.at[0], ql_recv.at[own], sibling)
 

time: 44.7 us -> 44.7 us (level)
  no operation moved by 1% of the time
where the time goes in v12:
time: 44.7 us; the launch traced here: 44.5 us
  Pallas kernels  43.1 us (96%)
  other arithmetic  1.29 us (3%)
    pallas_call x1, Pallas kernels, shards(): pl.pallas_call(kernel, out_shape=jax.ShapeDtypeStruct((4, 448), F32), in_...  43.1 us
    convert_element_type x1, other arithmetic, shards(): return pl.pallas_call(kernel, out_shape=jax.ShapeDtypeStruct((4, 448), F3...  1.29 us

profile of v12, /device:TPU:8, one launch (start us, length us, event | category | flops | bytes accessed | tf_op | source)
XLA Modules:
  0.0 44.5 jit_solution(6534477995934266068)
XLA Ops:
  0.0 43.1 %shard_map.91 = f32[4,448]{1,0:T(4,128)} custom-call(bf16[4,1536]{1,0:T(4,128)(2,1)} %ql_hbm.1, bf16[4,512]{1,0:T(4,128)(2,1)} %nl_hbm.1, bf16[4,64]{1,0:T(4,128)(2,1)} %nr_hbm.1, bf16[4,1024,512]{2,1,0:T(8,128)(2,1)} %lat_hbm.1, bf16[4,64,1024]{2,1,0:T(8,128)(2,1)} %bitcast.1, s32[4]{0:T(128)} %len_hbm.1, bf16[12,1536]{1,0:T(8,128)(2,1)} %qup_hbm.1, ...), custom_call_target="tpu_custom_call" | custom-call | flops 400000000 | bytes 5000000 | tf_op jit(solution)/shard_map/pallas_call | solution.py:440
  43.2 1.3 %convert_element_type.3 = bf16[4,448]{1,0:T(4,128)(2,1)} convert(f32[4,448]{1,0:T(4,128)} %shard_map.91) | non-fusion elementwise | flops 1792 | bytes 10752 | tf_op jit(solution)/shard_map/convert_element_type | solution.py:485
